TPU v7x, 128 devices: a whole 4x4x4 slice. The times are simulated.
128 devices in a mesh: dp: 8 (over x, core), ctx: 16 (over z, y).
Axes of the slice: x: 4, y: 4, z: 4, core: 2. Of those that a mesh axis runs over, the one named last changes fastest.
Arguments:
- layer_input: bfloat16 [8, 4096, 2048], P('dp', 'ctx'), may hold values from -6 to 6
- queries: bfloat16 [8, 4096, 1024], P('dp', 'ctx'), may hold values from -6 to 6
- gates: float32 [8, 4096, 8], P('dp', 'ctx'), may hold values from 0 to 1
- regularizer: float32 [8], replicated, may hold values from 0.25 to 1
- key_weight: bfloat16 [2048, 1024], replicated, may hold values from -0.0234375 to 0.0234375
- value_weight: bfloat16 [2048, 1024], replicated, may hold values from -0.125 to 0.125
- out_cotangent: bfloat16 [8, 4096, 1024], P('dp', 'ctx'), may hold values from -6 to 6
- lengths: int32 [8, 16], P('dp', 'ctx'), may hold values from 0 to 256, as said below
Outputs:
- input_grad: bfloat16 [8, 4096, 2048], P('dp', 'ctx')
- query_grad: float32 [8, 4096, 1024], P('dp', 'ctx')
- key_weight_grad: float32 [2048, 1024], P(('dp', 'ctx'))
- value_weight_grad: float32 [2048, 1024], P(('dp', 'ctx'))
Inputs may be any that keep to these rules, and one draw needn't show every extreme that they name: lengths[s, c] counts the valid tokens of block c of sequence s; the valid tokens of a sequence are its first ones, and at least half of 4096.
All inputs are finite; a program needn't handle non-finite values.
Results may differ from a plain program's by a relative error of at most 0.005.
Values sent between devices are 32-bit elements; how exact they have to be, the bound alone decides.
A program may use at most 128 MiB of HBM per device.

v0:
```python
import jax
import jax.numpy as jnp
from jax import lax
from jax.sharding import PartitionSpec as P

ITERS = 4


HIGHEST = lax.Precision.HIGHEST
tiny = 1e-06


def prefix(part, axis, combine, identity, reverse):
    count = lax.axis_size(axis)
    place = lax.axis_index(axis)
    ahead = count - 1 - place if reverse else place
    gathered = jax.tree.map(lambda a: lax.all_gather(a, axis), part)
    state = jax.tree.map(lambda a, e: jnp.zeros_like(a) + jnp.asarray(e, a.dtype), part, identity)

    def one(step, state):
        source = count - 1 - step if reverse else step
        return combine(
            state, jax.tree.map(lambda a: lax.dynamic_index_in_dim(a, source, 0, False), gathered)
        )

    return lax.fori_loop(0, ahead, one, state)


def contract(form, *operands):
    return jnp.einsum(form, *operands, precision=HIGHEST)


def decay_tables(gate_logarithm):
    running = jnp.cumsum(gate_logarithm, axis=0)
    heads_first = running.T
    log_gap = heads_first[:, :, None] - heads_first[:, None, :]
    tokens_len = gate_logarithm.shape[0]
    causal = jnp.arange(tokens_len)[:, None] >= jnp.arange(tokens_len)[None, :]
    decay_table = jnp.exp(jnp.where(causal[None], log_gap, -1e30))
    return (decay_table, jnp.exp(running), jnp.exp(running[-1:] - running), running[-1])


def apply_system(operand, key_rows, decay_table, start_w, key_gram, ridge):
    scores = contract("thd,shd->hts", operand, key_rows) * decay_table
    inner_part = contract("hts,shd->thd", scores, key_rows)
    outer_part = start_w[:, :, None] * contract("thd,hde->the", operand, key_gram)
    return ridge[None, :, None] * operand + outer_part + inner_part


def conj_grad(right_side, key_rows, decay_table, start_w, key_gram, ridge):
    solution = jnp.zeros_like(right_side)
    residual = right_side
    direction = right_side
    norm_now = jnp.sum(residual * residual, axis=-1)
    for iteration in range(ITERS):
        image_vec = apply_system(direction, key_rows, decay_table, start_w, key_gram, ridge)
        step_size = norm_now / (jnp.sum(direction * image_vec, axis=-1) + tiny)
        solution = solution + step_size[..., None] * direction
        residual = residual - step_size[..., None] * image_vec
        norm_next = jnp.sum(residual * residual, axis=-1)
        direction = residual + (norm_next / (norm_now + tiny))[..., None] * direction
        norm_now = norm_next
    return solution


def block_solves(
    key_rows, value_rows, query_rows, cot_rows, decay_table, start_w, key_gram, value_key, ridge
):
    solution = conj_grad(query_rows, key_rows, decay_table, start_w, key_gram, ridge)
    value_scores = contract("thv,shv->hts", cot_rows, value_rows) * decay_table
    right_side = start_w[:, :, None] * contract("thv,hvd->thd", cot_rows, value_key)
    right_side = right_side + contract("hts,shd->thd", value_scores, key_rows)
    adjoint = conj_grad(right_side, key_rows, decay_table, start_w, key_gram, ridge)
    return (solution, adjoint, value_scores)


def local_states(key_rows, value_rows, end_w):
    return (
        contract("sh,shd,she->hde", end_w, key_rows, key_rows),
        contract("sh,shv,shd->hvd", end_w, value_rows, key_rows),
    )


def back_states(solution, adjoint, cot_rows, start_w):
    cross = contract("th,thd,the->hde", start_w, adjoint, solution)
    return (
        -(cross + jnp.swapaxes(cross, 1, 2)),
        contract("th,thv,thd->hvd", start_w, cot_rows, solution),
    )


def block_grads(
    key_rows,
    value_rows,
    solution,
    adjoint,
    cot_rows,
    value_scores,
    decay_table,
    end_w,
    sym_back,
    pair_back,
):
    sol_scores = contract("thd,shd->hts", solution, key_rows) * decay_table
    adj_scores = contract("thd,shd->hts", adjoint, key_rows) * decay_table
    key_grad = contract("hts,thd->shd", value_scores, solution)
    key_grad = key_grad - contract("hts,thd->shd", sol_scores, adjoint)
    key_grad = key_grad - contract("hts,thd->shd", adj_scores, solution)
    carried = contract("shd,hde->she", key_rows, sym_back) + contract(
        "shv,hvd->shd", value_rows, pair_back
    )
    key_grad = key_grad + end_w[:, :, None] * carried
    value_grad = contract("hts,thv->shv", sol_scores, cot_rows)
    value_grad = value_grad + end_w[:, :, None] * contract("shd,hvd->shv", key_rows, pair_back)
    return (key_grad, value_grad)


def prepare(block_input, block_queries, block_gates, block_cot, length, key_weight, value_weight):
    tokens_len = block_input.shape[0]
    heads = block_gates.shape[1]
    valid_mask = (jnp.arange(tokens_len, dtype=jnp.int32) < length).astype(jnp.float32)[
        :, None, None
    ]
    key_rows = (
        jnp.dot(block_input, key_weight, preferred_element_type=jnp.float32).reshape(
            tokens_len, heads, -1
        )
        * valid_mask
    )
    value_rows = (
        jnp.dot(block_input, value_weight, preferred_element_type=jnp.float32).reshape(
            tokens_len, heads, -1
        )
        * valid_mask
    )
    query_rows = block_queries.astype(jnp.float32).reshape(tokens_len, heads, -1)
    cot_rows = block_cot.astype(jnp.float32).reshape(tokens_len, heads, -1) * valid_mask
    return (valid_mask, key_rows, value_rows, query_rows, cot_rows)


def combine_states(earlier, later):
    factor_early, gram_early, pair_early = earlier
    factor_late, gram_late, pair_late = later
    scale = factor_late[..., None, None]
    return (
        factor_early * factor_late,
        scale * gram_early + gram_late,
        scale * pair_early + pair_late,
    )


def body(
    layer_input, queries, gates, regularizer, key_weight, value_weight, out_cotangent, lengths
):

    def local_part(block_input, block_queries, block_gates, block_cot, length):
        valid_mask, key_rows, value_rows, query_rows, cot_rows = prepare(
            block_input, block_queries, block_gates, block_cot, length, key_weight, value_weight
        )
        decay_table, start_w, end_w, block_total = decay_tables(jnp.log(block_gates))
        gram_local, pair_local = local_states(key_rows, value_rows, end_w)
        return (
            valid_mask,
            key_rows,
            value_rows,
            query_rows,
            cot_rows,
            decay_table,
            start_w,
            end_w,
            block_total,
            gram_local,
            pair_local,
        )

    (
        valid_mask,
        key_rows,
        value_rows,
        query_rows,
        cot_rows,
        decay_table,
        start_w,
        end_w,
        block_total,
        gram_local,
        pair_local,
    ) = jax.vmap(local_part)(layer_input, queries, gates, out_cotangent, lengths[:, 0])
    block_factor = jnp.exp(block_total)
    identity = (jnp.ones_like(block_factor), jnp.zeros_like(gram_local), jnp.zeros_like(pair_local))
    _, key_gram, value_key = prefix(
        (block_factor, gram_local, pair_local), "ctx", combine_states, identity, False
    )
    solution, adjoint, value_scores = jax.vmap(
        block_solves, in_axes=(0, 0, 0, 0, 0, 0, 0, 0, None)
    )(
        key_rows,
        value_rows,
        query_rows,
        cot_rows,
        decay_table,
        start_w,
        key_gram,
        value_key,
        regularizer,
    )
    sym_local, back_pair = jax.vmap(back_states)(solution, adjoint, cot_rows, start_w)
    _, sym_back, pair_back = prefix(
        (block_factor, sym_local, back_pair), "ctx", combine_states, identity, True
    )
    key_grad, value_grad = jax.vmap(block_grads)(
        key_rows,
        value_rows,
        solution,
        adjoint,
        cot_rows,
        value_scores,
        decay_table,
        end_w,
        sym_back,
        pair_back,
    )
    batch_rows, tokens_len = (layer_input.shape[0], layer_input.shape[1])
    head_width = key_weight.shape[1]
    key_flat = (
        (key_grad * valid_mask).reshape(batch_rows * tokens_len, head_width).astype(jnp.bfloat16)
    )
    value_flat = (
        (value_grad * valid_mask).reshape(batch_rows * tokens_len, head_width).astype(jnp.bfloat16)
    )
    flat_input = layer_input.reshape(batch_rows * tokens_len, -1)
    dims = (((1,), (1,)), ((), ()))
    input_grad = lax.dot_general(key_flat, key_weight, dims, preferred_element_type=jnp.float32)
    input_grad = input_grad + lax.dot_general(
        value_flat, value_weight, dims, preferred_element_type=jnp.float32
    )
    input_grad = input_grad.astype(jnp.bfloat16).reshape(batch_rows, tokens_len, -1)
    query_grad = adjoint.reshape(batch_rows, tokens_len, head_width)
    grad_rows = jnp.concatenate([key_flat, value_flat], axis=1)
    summed = lax.psum_scatter(
        lax.dot_general(
            flat_input, grad_rows, (((0,), (0,)), ((), ())), preferred_element_type=jnp.float32
        ),
        ("dp", "ctx"),
        scatter_dimension=0,
        tiled=True,
    )
    return (input_grad, query_grad, summed[:, :head_width], summed[:, head_width:])


def solution(mesh):
    in_specs = (
        P("dp", "ctx", None),
        P("dp", "ctx", None),
        P("dp", "ctx", None),
        P(),
        P(),
        P(),
        P("dp", "ctx", None),
        P("dp", "ctx"),
    )
    out_specs = (
        P("dp", "ctx", None),
        P("dp", "ctx", None),
        P(("dp", "ctx"), None),
        P(("dp", "ctx"), None),
    )
    return jax.shard_map(body, mesh=mesh, in_specs=in_specs, out_specs=out_specs, check_vma=False)
```

profile of v0, /device:TPU:0, one launch (start us, length us, event | category | flops | bytes accessed | tf_op | source)
XLA Modules:
  0.0 1105.8 jit_solution(403251244335445375)
XLA Ops:
  9.8 6.5 copy.394
  16.3 6.5 copy.393
  22.8 3.6 convolution_multiply_fusion
  41.6 22.4 %all_gather.30 = f32[16,1,8]{2,1,0:T(1,128)S(1)} all-gather(f32[1,1,8]{2,1,0:T(1,128)S(1)} %copy.235), channel_id=1, replica_groups=mesh['dp'=8,'ctx'=16] {'ctx'}, dimensions={0}, use_global_device_ids=true | all-gather | bytes 544 | tf_op jit(solution)/shard_map/all_gather | solution.py:17
  65.2 5.0 fusion.52
  70.2 34.1 %all-gather.11.cloned.1.call-done = f32[128,128,128]{2,1,0:T(8,128)} async-done(((f32[8,128,128]{2,1,0:T(8,128)}), f32[128,128,128]{2,1,0:T(8,128)}) %all-gather.11.cloned.1.call-update) | async-done | bytes 8388624 | tf_op jit(solution)/shard_map/all_gather | solution.py:17
  104.3 72.6 %all-gather.9.cloned.1.call-done = f32[128,128,128]{2,1,0:T(8,128)} async-done(((f32[8,128,128]{2,1,0:T(8,128)}), f32[128,128,128]{2,1,0:T(8,128)}) %all-gather.9.cloned.1.call-update) | async-done | bytes 8388624 | tf_op jit(solution)/shard_map/all_gather | solution.py:17
  183.8 4.0 fusion.25
  192.8 4.0 fusion.28
  201.9 4.0 fusion.31
  213.2 3.8 fusion.22
  217.1 3.5 convolution_bitcast_fusion.2
  223.7 4.1 fusion.34
  232.7 4.0 fusion.37
  241.7 4.0 fusion.40
  251.0 4.0 fusion.43
  278.3 4.1 fusion.49
  282.5 23.8 %all-gather.15.cloned.1.call-done = f32[128,128,128]{2,1,0:T(8,128)} async-done(((f32[8,128,128]{2,1,0:T(8,128)}), f32[128,128,128]{2,1,0:T(8,128)}) %all-gather.15.cloned.1.call-update) | async-done | bytes 8388624 | tf_op jit(solution)/shard_map/all_gather | solution.py:17
  306.2 72.5 %all-gather.13.cloned.1.call-done = f32[16,8,128,128]{3,2,1,0:T(8,128)} async-done(((f32[1,8,128,128]{3,2,1,0:T(8,128)}), f32[16,8,128,128]{3,2,1,0:T(8,128)}) %all-gather.13.cloned.1.call-update) | async-done | bytes 8388624 | tf_op jit(solution)/shard_map/all_gather | solution.py:17
  378.8 23.9 %while.31 = (s32[]{:T(128)}, f32[1,8,128,128]{3,2,1,0:T(8,128)S(1)}, f32[1,8,128,128]{3,2,1,0:T(8,128)S(1)}, s32[]{:T(128)}, f32[16,1,8]{2,1,0:T(1,128)S(1)}, /*...) while((s32[]{:T(128)}, ...), condition=%wide.region_21.22_spmd, body=%wide.region_20.21_spmd.sunk | while | flops 524294 | bytes 3145995 | solution.py:26
  406.6 8.1 convolution_bitcast_fusion
  414.6 17.6 %copy.395 = f32[2048,2048]{1,0:T(8,128)} copy(f32[2048,2048]{0,1:T(8,128)} %convolution_bitcast_fusion) | data formatting | bytes 33554432
  435.1 3.7 fusion.210
  441.1 656.5 %reduce-scatter.4.cloned.1.call-done = f32[16,2048]{1,0:T(8,128)} async-done(((f32[2048,2048]{1,0:T(8,128)}), f32[16,2048]{1,0:T(8,128)}) %reduce-scatter.4.cloned.1.call-update) | async-done | bytes 131088
  (178 shorter events, 117.8 us)
Async XLA Ops:
  7.2 15.6 %copy-start = (bf16[1,256,2048]{2,1,0:T(8,128)(2,1)S(1)}, bf16[1,256,2048]{2,1,0:T(8,128)(2,1)}, u32[]{:S(2)}) copy-start(bf16[1,256,2048]{2,1,0:T(8,128)(2,1)} %param.12) | copy-start | bytes 3145732
  7.2 97.1 %all-gather.11.cloned.1.call-start = ((), (), s32[]{:S(2)}) async-start(), calls=%async_computation.2 | async-start | bytes 8912896 | tf_op jit(solution)/shard_map/all_gather | solution.py:17
  22.8 3.6 copy-start.17
  26.4 1.3 copy-start.12
  30.8 3.2 copy-start.21
  30.8 146.1 %all-gather.9.cloned.1.call-start = ((), (), s32[]{:S(2)}) async-start(), calls=%async_computation.1 | async-start | bytes 8912896 | tf_op jit(solution)/shard_map/all_gather | solution.py:17
  33.9 272.3 %all-gather.15.cloned.1.call-start = ((), (), s32[]{:S(2)}) async-start(), calls=%async_computation.4 | async-start | bytes 8912896 | tf_op jit(solution)/shard_map/all_gather | solution.py:17
  37.8 26.4 %copy-start.14 = (bf16[32,8,8,128]{3,2,1,0:T(8,128)(2,1)}, bf16[32,8,8,128]{3,2,1,0:T(8,128)(2,1)S(1)}, u32[]{:S(2)}) copy-start(bf16[32,8,8,128]{3,2,1,0:T(8,128)(2,1)S(1)} %copy.399) | copy-start | bytes 1572868
  177.7 2.8 copy-start.1
  207.3 2.4 copy-start.4
  212.7 166.0 %all-gather.13.cloned.1.call-start = ((), (), s32[]{:S(2)}) async-start(), calls=%async_computation.3 | async-start | bytes 8912896 | tf_op jit(solution)/shard_map/all_gather | solution.py:17
  217.0 3.6 copy-start.10
  217.0 3.6 copy-start.5
  256.4 2.3 copy-start.3
  265.8 831.7 %reduce-scatter.4.cloned.1.call-start = ((), (), s32[]{:S(2)}) async-start(), calls=%async_computation.5 | async-start | bytes 16908288
  266.1 2.2 copy-start.6
  268.2 3.4 copy-start.8
  271.7 1.9 copy-start.11
  403.8 1.3 copy-start.13
  403.8 1.6 copy-start.18
  406.5 8.1 copy-start.19
  433.8 1.3 copy-start.20
  435.1 3.7 copy-start.16
  435.1 3.7 copy-start.23
  (6 other events, 6.4 us)
Sparse Core Ops, SparseCore 0:
  31.0 73.3 all-gather.10
  106.5 70.4 all-gather.8
  212.9 93.3 all-gather.14
  308.2 70.4 all-gather.12
  432.4 665.1 reduce-scatter.3
where the time goes:
time: 1110 us
  waiting for transfers between devices  860 us (77%)
  matrix products  120 us (11%)
  local copies, waits for them, and re-layouts  47.4 us (4%)
  other arithmetic  39.5 us (4%)
  blocking collectives  22.4 us (2%)
  between operations  15.4 us (1%)
    unnamed x6, waiting for transfers between devices  657 us
    all_gather x4, waiting for transfers between devices, prefix(): gathered = jax.tree.map(lambda a: lax.all_gather(a, axis), part)  203 us
    dot_general x40, matrix products, contract(): return jnp.einsum(form, *operands, precision=HIGHEST)  101 us
    unnamed x55, local copies, waits for them, and re-layouts  25.4 us
    add x15, other arithmetic, combine_states(): scale * pair_early + pair_late  23.3 us
    all_gather x1, blocking collectives, prefix(): gathered = jax.tree.map(lambda a: lax.all_gather(a, axis), part)  22.4 us
  transfers between devices with their start and end apart: 5, of which 5 were waited for; matrix products, arithmetic and copies ran while one was open for 8% of the time, Pallas kernels for 0%

commit v1 on v0

v1 whole, which is shorter than its diff:
```python
import functools

import jax
import jax.numpy as jnp
from jax import lax
from jax.experimental import pallas as pl
from jax.experimental.pallas import tpu as pltpu
from jax.sharding import PartitionSpec as P

ITERS = 4
TINY = 1e-06
DK = 128
PAIR = 2
F32 = jnp.float32
BF16 = jnp.bfloat16
MESH = pl.DeviceIdType.MESH


def split(a):
    high = a.astype(BF16)
    return high, (a - high.astype(F32)).astype(BF16)


def dot(a, b):
    return jnp.dot(a, b, preferred_element_type=F32)


def left3(parts):
    high, low = parts
    return jnp.concatenate([high, low, high], axis=1)


def right3(parts):
    high, low = parts
    return jnp.concatenate([high, high, low], axis=0)


def dot3(a, b):
    return dot(left3(a), right3(b))


def mesa_kernel(
    sizes,
    x_ref, q_ref, gates_ref, reg_ref, wk_ref, wv_ref, g_ref, len_ref,
    ig_ref, qg_ref, kwg_ref, vwg_ref,
    x_s, w_s, q_s, g_s, gate_s, run_s, tot_s, sw_s, ew_s, fac_snd, fac_rcv,
    kv_s, kt_s, dt_s, vs_s, rhs_s, ewc_s, loc_s,
    snd1, rcv1, rcv2, snd3, rcv3, rcv4,
    xs_snd, xs_rcv, xt_s, gr_s, sib_snd, sib_rcv, wp_s,
    ra1, ra2, ra3, rb1, rb2, rb3, rc1, rc2, rc3,
    ld_sem, w_sem, fac_sem, x_sem, sib_sem, s1, r1, s2, r2, s3, r3, s4, r4, rs_snd, rs_rcv,
):
    nx, nz, ny, heads, tokens, width = sizes
    nctx = nz * ny
    groups = heads // PAIR
    srows = DK // nctx
    xb = width // (2 * nx)
    rows = xb // nctx
    half = rows // 2
    dp, ctx = lax.axis_index("dp"), lax.axis_index("ctx")
    mx, mc = lax.div(dp, 2), lax.rem(dp, 2)
    mz, my = lax.div(ctx, ny), lax.rem(ctx, ny)
    sib = mx * 2 + (1 - mc)

    barrier = pltpu.get_barrier_semaphore()
    for o in range(1, nctx):
        pl.semaphore_signal(barrier, inc=1, device_id=(dp, lax.rem(ctx + o, nctx)), device_id_type=MESH)
    pl.semaphore_signal(barrier, inc=1, device_id=(sib, ctx), device_id_type=MESH)
    for o in range(1, nx):
        pl.semaphore_signal(
            barrier, inc=1, device_id=(lax.rem(mx + o, nx) * 2 + mc, ctx), device_id_type=MESH
        )

    pltpu.make_async_copy(x_ref.at[0], x_s, ld_sem.at[0]).start()
    for h in range(heads):
        cols = pl.ds(h * DK, DK)
        pltpu.make_async_copy(wk_ref.at[:, cols], w_s.at[h, :, pl.ds(0, DK)], w_sem.at[h]).start()
        pltpu.make_async_copy(wv_ref.at[:, cols], w_s.at[h, :, pl.ds(DK, DK)], w_sem.at[h]).start()
    for h in range(heads):
        cols = pl.ds(h * DK, DK)
        pltpu.make_async_copy(g_ref.at[0, :, cols], g_s.at[h], ld_sem.at[1]).start()
        pltpu.make_async_copy(q_ref.at[0, :, cols], q_s.at[h], ld_sem.at[2]).start()

    length = len_ref[0, 0]
    gate_s[...] = jnp.ones_like(gate_s)
    gate_s[:, 0:heads] = gates_ref[0]
    run = jnp.log(gate_s[...].T[0:heads])
    lane = lax.broadcasted_iota(jnp.int32, (heads, tokens), 1)
    step = 1
    while step < tokens:
        run = run + jnp.where(lane >= step, pltpu.roll(run, step, 1), 0.0)
        step *= 2
    total = jnp.broadcast_to(run[:, tokens - 1 : tokens], (heads, tokens))
    run_s[...] = run
    tot_s[...] = total
    sw_s[...] = jnp.exp(run)
    ew_s[...] = jnp.exp(total - run)
    fac_snd[...] = jnp.exp(total)

    mask_rows = (lax.broadcasted_iota(jnp.int32, (tokens, 2 * DK), 0) < length).astype(F32)
    mask_lane = (lax.broadcasted_iota(jnp.int32, (1, tokens), 1) < length).astype(F32)

    def all_to_all(src, dst, g, send, recv):
        for o in range(1, nctx):
            to = lax.rem(ctx + o, nctx)
            pltpu.make_async_remote_copy(
                src_ref=src.at[g, to], dst_ref=dst.at[g, ctx], send_sem=send.at[g], recv_sem=recv.at[g],
                device_id=(dp, to), device_id_type=MESH,
            ).start()
        pltpu.make_async_copy(src.at[g, ctx], dst.at[g, ctx], recv.at[g]).start()

    def wait_all(buf, sem):
        pltpu.make_async_copy(buf, buf, sem).wait()

    def wait_sent(buf, g, sem):
        part = buf.at[g, pl.ds(0, nctx - 1)]
        pltpu.make_async_copy(part, part, sem.at[g]).wait()

    def project(g):
        for i in range(PAIR):
            h = g * PAIR + i
            wait_all(w_s.at[h], w_sem.at[h])
            kv = dot(x_s[...], w_s[h]) * mask_rows
            parts = split(kv)
            kv_s[h, 0], kv_s[h, 1] = parts
            kt = kv[:, 0:DK].T
            kt_s[h, 0], kt_s[h, 1] = split(kt)
            state = dot3(split(kt * ew_s[pl.ds(h, 1), :]), parts)
            snd1[g, :, i] = state.reshape(nctx, srows, 2 * DK)

    def tables(g):
        for i in range(PAIR):
            h = g * PAIR + i
            run_row = run_s[pl.ds(h, 1), :]
            run_col = jnp.broadcast_to(run_row, (DK, tokens)).T
            ewc_s[h] = jnp.exp(tot_s[pl.ds(h, 1), :][:, 0:DK] - run_col)
            gap = run_row - jnp.concatenate([run_col] * (tokens // DK), axis=1)
            later = lax.broadcasted_iota(jnp.int32, (tokens, tokens), 1) >= lax.broadcasted_iota(
                jnp.int32, (tokens, tokens), 0
            )
            table = jnp.exp(jnp.where(later, gap, -1e30))
            dt_s[h] = table
            gt = ((g_s[h].astype(F32)).T * mask_lane).astype(BF16)
            v_both = jnp.concatenate([kv_s[h, 0, :, DK:], kv_s[h, 1, :, DK:]], axis=1)
            scores = dot(v_both, jnp.concatenate([gt, gt], axis=0)) * table
            vs_s[h] = scores
            rhs_s[h] = dot3((kt_s[h, 0], kt_s[h, 1]), split(scores))

    def prefix(buf, g, order):
        held = [jnp.zeros((srows, 2 * DK), F32) for _ in range(PAIR)]
        for c in order:
            for i in range(PAIR):
                mine = buf[g, c, i]
                buf[g, c, i] = held[i]
                held[i] = fac_rcv[c, pl.ds(g * PAIR + i, 1), :] * held[i] + mine

    def solve(g):
        state = [rcv2[g, :, i].reshape(DK, 2 * DK) for i in range(PAIR)]
        x, r, p, rr, keys, kts, big, gts = ([None] * PAIR for _ in range(8))
        for i in range(PAIR):
            h = g * PAIR + i
            qt = q_s[h].astype(F32).T
            gts[i] = ((g_s[h].astype(F32)).T * mask_lane).astype(BF16)
            gram, pair = split(state[i][:, 0:DK]), split(state[i][:, DK:])
            right = rhs_s[h] + sw_s[pl.ds(h, 1), :] * dot(
                jnp.concatenate(pair, axis=1), jnp.concatenate([gts[i], gts[i]], axis=0)
            )
            p[i] = r[i] = jnp.concatenate([qt, right], axis=1)
            rr[i] = jnp.sum(r[i] * r[i], axis=0, keepdims=True)
            keys[i] = (kv_s[h, 0, :, 0:DK], kv_s[h, 1, :, 0:DK])
            kts[i] = (kt_s[h, 0], kt_s[h, 1])
            big[i] = tuple(jnp.concatenate([a, b], axis=0) for a, b in zip(keys[i], gram))
        for it in range(ITERS):
            last = it == ITERS - 1
            for i in range(PAIR):
                h = g * PAIR + i
                table = jnp.concatenate([dt_s[h]] * 2, axis=1)
                sw = jnp.concatenate([sw_s[pl.ds(h, 1), :]] * 2, axis=1)
                if last:
                    both = dot(big[i][0], p[i].astype(BF16))
                    inner = dot(kts[i][0], (both[0:tokens] * table).astype(BF16))
                else:
                    both = dot3(big[i], split(p[i]))
                    inner = dot3(kts[i], split(both[0:tokens] * table))
                image = reg_ref[h] * p[i] + sw * both[tokens:] + inner
                size = rr[i] / (jnp.sum(p[i] * image, axis=0, keepdims=True) + TINY)
                x[i] = size * p[i] if it == 0 else x[i] + size * p[i]
                if not last:
                    r[i] = r[i] - size * image
                    following = jnp.sum(r[i] * r[i], axis=0, keepdims=True)
                    p[i] = r[i] + (following / (rr[i] + TINY)) * p[i]
                    rr[i] = following
        for i in range(PAIR):
            h = g * PAIR + i
            xt, yt = x[i][:, 0:tokens], x[i][:, tokens:]
            xn, yn = xt.T, yt.T
            qg_ref[0, :, pl.ds(pl.multiple_of(h * DK, DK), DK)] = yn
            gn = (g_s[h].astype(F32) * mask_rows[:, 0:DK]).astype(BF16)
            y_high, y_low = split(yn)
            yg = (
                jnp.concatenate([y_high, gn], axis=1),
                jnp.concatenate([y_low, jnp.zeros_like(gn)], axis=1),
            )
            back = dot3(split(xt * sw_s[pl.ds(h, 1), :]), yg)
            snd3[g, :, i] = back.reshape(nctx, srows, 2 * DK)
            table = jnp.concatenate([dt_s[h]] * 2, axis=1)
            scores = dot3(keys[i], split(x[i])) * table
            sol, adj = scores[:, 0:tokens], scores[:, tokens:]
            from_x = dot3(split(vs_s[h] - adj), split(xn))
            from_yg = dot3(split(sol), yg)
            loc_s[h] = jnp.concatenate([from_x - from_yg[:, 0:DK], from_yg[:, DK:]], axis=1)

    def gradients(g):
        for i in range(PAIR):
            h = g * PAIR + i
            state = rcv4[g, :, i].reshape(DK, 2 * DK)
            cross, pair_t = state[:, 0:DK], state[:, DK:]
            sym, pair = -(cross + cross.T), pair_t.T
            both = jnp.concatenate(
                [
                    jnp.concatenate([sym, pair_t], axis=1),
                    jnp.concatenate([pair, jnp.zeros_like(pair)], axis=1),
                ],
                axis=0,
            )
            carried = dot3((kv_s[h, 0], kv_s[h, 1]), split(both))
            decay = jnp.concatenate([ewc_s[h]] * 2, axis=1)
            grad = ((loc_s[h] + decay * carried) * mask_rows).astype(BF16)
            gr_s[g, 0:tokens, pl.ds(i * 2 * DK, 2 * DK)] = grad
            sib_snd[g, :, pl.ds(i * 2 * DK, 2 * DK)] = grad.astype(F32)

    def sib_copy(g):
        return pltpu.make_async_remote_copy(
            src_ref=sib_snd.at[g], dst_ref=sib_rcv.at[g], send_sem=sib_sem.at[0, g], recv_sem=sib_sem.at[1, g],
            device_id=(sib, ctx), device_id_type=MESH,
        )

    me = {"x": mx, "z": mz, "y": my}
    count = {"x": nx, "z": nz, "y": ny}
    lanes3, lanes1 = pl.ds(0, 3 * DK), pl.ds(3 * DK, DK)
    parts = (
        ("xyz", pl.ds(0, half), lanes3, (ra1, ra2, ra3)),
        ("yzx", pl.ds(half, half), lanes3, (rb1, rb2, rb3)),
        ("zxy", pl.ds(0, rows), lanes1, (rc1, rc2, rc3)),
    )

    def device(axis, at):
        place = dict(me)
        place[axis] = at
        return (place["x"] * 2 + mc, place["z"] * ny + place["y"])

    def chunk(n, part, g, at):
        order, rws, lns, bufs = parts[part]
        left = [a for a in "xzy" if a not in order[:n]]
        spot = tuple(at if a == order[n] else slice(None) for a in left)
        if n == 0:
            return wp_s.at[(g,) + spot + (rws, lns)]
        return bufs[n - 1].at[(g, 0) + spot]

    def scatter_start(n, g):
        for part, (order, rws, lns, bufs) in enumerate(parts):
            axis = order[n]
            for o in range(1, count[axis]):
                to = lax.rem(me[axis] + o, count[axis])
                pltpu.make_async_remote_copy(
                    src_ref=chunk(n, part, g, to), dst_ref=bufs[n].at[g, o - 1],
                    send_sem=rs_snd.at[part, n, g], recv_sem=rs_rcv.at[part, n, g],
                    device_id=device(axis, to), device_id_type=MESH,
                ).start()

    def scatter_add(n, g):
        for part, (order, rws, lns, bufs) in enumerate(parts):
            wait_all(bufs[n].at[g], rs_rcv.at[part, n, g])
            summed = chunk(n, part, g, me[order[n]])[...]
            for o in range(count[order[n]] - 1):
                summed = summed + bufs[n][g, o]
            if n < 2:
                bufs[n][g, 0] = summed
            else:
                first = pl.ds(pl.multiple_of(g * PAIR * DK, DK), DK)
                second = pl.ds(pl.multiple_of(g * PAIR * DK + DK, DK), DK)
                if part < 2:
                    kwg_ref[rws, first] = summed[:, 0:DK]
                    vwg_ref[rws, first] = summed[:, DK : 2 * DK]
                    kwg_ref[rws, second] = summed[:, 2 * DK :]
                else:
                    vwg_ref[rws, second] = summed

    def weight_part(g):
        sib_copy(g).wait_recv()
        gr_s[g, tokens:, :] = sib_rcv[g].astype(BF16)
        for k in range(nx):
            out = dot(xt_s[k * xb : (k + 1) * xb, :], gr_s[g])
            wp_s[g, k] = out.reshape(nz, ny, rows, PAIR * 2 * DK)
        scatter_start(0, g)

    def input_gradient():
        def columns(n, carry):
            span = pl.ds(pl.multiple_of(n * 256, 256), 256)
            total = None
            for h in range(heads):
                grad = gr_s[h // PAIR, 0:tokens, (h % PAIR) * 2 * DK : (h % PAIR + 1) * 2 * DK]
                term = lax.dot_general(
                    grad, w_s[h, span, :], (((1,), (1,)), ((), ())), preferred_element_type=F32
                )
                total = term if total is None else total + term
            ig_ref[0, :, span] = total.astype(BF16)
            return carry

        lax.fori_loop(0, width // 256, columns, 0)

    wait_all(x_s, ld_sem.at[0])
    project(0)
    pl.semaphore_wait(barrier, nctx - 1 + 1 + nx - 1)
    for o in range(1, nctx):
        to = lax.rem(ctx + o, nctx)
        pltpu.make_async_remote_copy(
            src_ref=fac_snd, dst_ref=fac_rcv.at[ctx], send_sem=fac_sem.at[0], recv_sem=fac_sem.at[1],
            device_id=(dp, to), device_id_type=MESH,
        ).start()
    pltpu.make_async_copy(fac_snd, fac_rcv.at[ctx], fac_sem.at[1]).start()
    all_to_all(snd1, rcv1, 0, s1, r1)

    def project_next(g, carry):
        project(g)
        all_to_all(snd1, rcv1, g, s1, r1)
        return carry

    lax.fori_loop(1, groups, project_next, 0)

    for k in range(nx):
        theirs = pl.ds(pl.multiple_of(k * 2 * xb + (1 - mc) * xb, xb), xb)
        xs_snd[:, k * xb : (k + 1) * xb] = x_s[:, theirs].astype(F32)
    x_copy = pltpu.make_async_remote_copy(
        src_ref=xs_snd, dst_ref=xs_rcv, send_sem=x_sem.at[0], recv_sem=x_sem.at[1],
        device_id=(sib, ctx), device_id_type=MESH,
    )
    x_copy.start()
    wait_all(g_s, ld_sem.at[1])
    wait_all(q_s, ld_sem.at[2])

    def tables_next(g, carry):
        tables(g)
        return carry

    lax.fori_loop(0, groups, tables_next, 0)
    for k in range(nx):
        mine = pl.ds(pl.multiple_of(k * 2 * xb + mc * xb, xb), xb)
        xt_s[k * xb : (k + 1) * xb, 0:tokens] = x_s[:, mine].astype(F32).T.astype(BF16)
    x_copy.wait_recv()
    for k in range(nx):
        xt_s[k * xb : (k + 1) * xb, tokens:] = xs_rcv[:, k * xb : (k + 1) * xb].T.astype(BF16)
    wait_all(fac_rcv, fac_sem.at[1])

    def during(s, first, fn):
        @pl.when(jnp.logical_and(s >= first, s < first + groups))
        def _():
            fn(s - first)

    def forward_prefix(g):
        wait_all(rcv1.at[g], r1.at[g])
        prefix(rcv1, g, range(nctx))
        all_to_all(rcv1, rcv2, g, s2, r2)

    def solves(g):
        wait_all(rcv2.at[g], r2.at[g])
        solve(g)
        all_to_all(snd3, rcv3, g, s3, r3)

    def backward_grads(g):
        wait_all(rcv4.at[g], r4.at[g])
        gradients(g)
        sib_copy(g).start()

    def backward_prefix(g):
        wait_all(rcv3.at[g], r3.at[g])
        prefix(rcv3, g, range(nctx - 1, -1, -1))
        all_to_all(rcv3, rcv4, g, s4, r4)

    def reduce_two(g):
        scatter_add(0, g)
        scatter_start(1, g)

    def reduce_three(g):
        scatter_add(1, g)
        scatter_start(2, g)

    def reduce_last(g):
        scatter_add(2, g)

    def one(s, carry):
        during(s, 0, forward_prefix)
        during(s, 1, solves)
        during(s, 3, backward_grads)
        during(s, 2, backward_prefix)
        during(s, 3, weight_part)
        pl.when(s == groups + 3)(input_gradient)
        during(s, 6, reduce_last)
        during(s, 5, reduce_three)
        during(s, 4, reduce_two)
        return carry

    lax.fori_loop(0, groups + 6, one, 0)

    sent = pltpu.make_async_copy(
        fac_rcv.at[pl.ds(0, nctx - 1)], fac_rcv.at[pl.ds(0, nctx - 1)], fac_sem.at[0]
    )
    sent.wait()
    x_copy.wait_send()

    def drain(g, carry):
        wait_sent(snd1, g, s1)
        wait_sent(rcv1, g, s2)
        wait_sent(snd3, g, s3)
        wait_sent(rcv3, g, s4)
        sib_copy(g).wait_send()
        for part in range(3):
            for n in range(3):
                buf = parts[part][3][n].at[g]
                wait_all(buf, rs_snd.at[part, n, g])
        return carry

    lax.fori_loop(0, groups, drain, 0)


def solution(mesh):
    nx = mesh.shape["dp"] // 2
    nctx = mesh.shape["ctx"]
    nz = ny = {16: 4, 4: 2}[nctx]

    def body(layer_input, queries, gates, regularizer, key_weight, value_weight, out_cotangent, lengths):
        tokens, width = layer_input.shape[1:]
        heads = gates.shape[2]
        groups = heads // PAIR
        rows = width // (2 * nx * nctx)
        srows = DK // nctx
        wide = PAIR * 2 * DK
        state = lambda: pltpu.VMEM((groups, nctx, PAIR, srows, 2 * DK), F32)
        dma = lambda *shape: pltpu.SemaphoreType.DMA(shape)
        scratch = [
            pltpu.VMEM((tokens, width), BF16),
            pltpu.VMEM((heads, width, 2 * DK), BF16),
            pltpu.VMEM((heads, tokens, DK), BF16),
            pltpu.VMEM((heads, tokens, DK), BF16),
            pltpu.VMEM((tokens, DK), F32),
            pltpu.VMEM((heads, tokens), F32),
            pltpu.VMEM((heads, tokens), F32),
            pltpu.VMEM((heads, tokens), F32),
            pltpu.VMEM((heads, tokens), F32),
            pltpu.VMEM((heads, 2 * DK), F32),
            pltpu.VMEM((nctx, heads, 2 * DK), F32),
            pltpu.VMEM((heads, 2, tokens, 2 * DK), BF16),
            pltpu.VMEM((heads, 2, DK, tokens), BF16),
            pltpu.VMEM((heads, tokens, tokens), F32),
            pltpu.VMEM((heads, tokens, tokens), F32),
            pltpu.VMEM((heads, DK, tokens), F32),
            pltpu.VMEM((heads, tokens, DK), F32),
            pltpu.VMEM((heads, tokens, 2 * DK), F32),
            state(), state(), state(), state(), state(), state(),
            pltpu.VMEM((tokens, width // 2), F32),
            pltpu.VMEM((tokens, width // 2), F32),
            pltpu.VMEM((width // 2, 2 * tokens), BF16),
            pltpu.VMEM((groups, 2 * tokens, wide), BF16),
            pltpu.VMEM((groups, tokens, wide), F32),
            pltpu.VMEM((groups, tokens, wide), F32),
            pltpu.VMEM((groups, nx, nz, ny, rows, wide), F32),
        ]
        count = {"x": nx, "z": nz, "y": ny}
        for order, rws, lns in (("xyz", rows // 2, 3 * DK), ("yzx", rows // 2, 3 * DK), ("zxy", rows, DK)):
            for n in range(3):
                left = tuple(count[a] for a in "xzy" if a not in order[: n + 1])
                scratch.append(pltpu.VMEM((groups, count[order[n]] - 1) + left + (rws, lns), F32))
        scratch += [dma(3), dma(heads), dma(2), dma(2), dma(2, groups)]
        scratch += [dma(groups)] * 8 + [dma(3, 3, groups)] * 2
        any_space = pl.BlockSpec(memory_space=pl.ANY)
        vmem = pl.BlockSpec(memory_space=pltpu.VMEM)
        smem = pl.BlockSpec(memory_space=pltpu.SMEM)
        return pl.pallas_call(
            functools.partial(mesa_kernel, (nx, nz, ny, heads, tokens, width)),
            out_shape=(
                jax.ShapeDtypeStruct((1, tokens, width), BF16),
                jax.ShapeDtypeStruct((1, tokens, heads * DK), F32),
                jax.ShapeDtypeStruct((rows, heads * DK), F32),
                jax.ShapeDtypeStruct((rows, heads * DK), F32),
            ),
            in_specs=[any_space, any_space, vmem, smem, any_space, any_space, any_space, smem],
            out_specs=(vmem, vmem, vmem, vmem),
            scratch_shapes=scratch,
            compiler_params=pltpu.CompilerParams(
                collective_id=0, has_side_effects=True, vmem_limit_bytes=63 << 20
            ),
            name="mesa_backward",
        )(layer_input, queries, gates, regularizer, key_weight, value_weight, out_cotangent, lengths)

    in_specs = (
        P("dp", "ctx", None),
        P("dp", "ctx", None),
        P("dp", "ctx", None),
        P(),
        P(),
        P(),
        P("dp", "ctx", None),
        P("dp", "ctx"),
    )
    out_specs = (
        P("dp", "ctx", None),
        P("dp", "ctx", None),
        P(("dp", "ctx"), None),
        P(("dp", "ctx"), None),
    )
    return jax.shard_map(body, mesh=mesh, in_specs=in_specs, out_specs=out_specs, check_vma=False)
```

time: 1110 us -> 123 us (0.11)
  waiting for transfers between devices: 860 us -> 0 us
  matrix products: 120 us -> 0 us
  Pallas kernels: 0 us -> 114 us
  local copies, waits for them, and re-layouts: 47.4 us -> 7.4 us
  other arithmetic: 39.5 us -> 0 us
  blocking collectives: 22.4 us -> 0 us
  between operations: 15.4 us -> 1.3 us
    unnamed x6 -> x0, waiting for transfers between devices: 657 us -> none
    all_gather x4 -> x0, waiting for transfers between devices: 203 us -> none  [prefix(): gathered = jax.tree.map(lambda a: lax.all_gather(a, axis), part)]
    dot_general x45 -> x0, matrix products: 120 us -> none  [the longest x40 101 us: contract(): return jnp.einsum(form, *operands, precision=HIGHEST)]
    pallas_call x0 -> x1, Pallas kernels: none -> 114 us  [body(): pl.pallas_call(functools.partial(mesa_kernel, (nx, nz, ny, heads, tokens,...]
    add x23 -> x0, other arithmetic: 30 us -> none  [the longest x15 23.3 us: combine_states(): scale * pair_early + pair_late]
    all_gather x1 -> x0, blocking collectives: 22.4 us -> none  [prefix(): gathered = jax.tree.map(lambda a: lax.all_gather(a, axis), part)]
    unnamed x55 -> x9, local copies, waits for them, and re-layouts: 25.4 us -> 7.4 us
    dot_general x3 -> x0, local copies, waits for them, and re-layouts: 15.1 us -> none  [the longest x1 6.52 us: prepare(): jnp.dot(block_input, key_weight, preferred_element_type=jnp.float32)]
  transfers between devices with their start and end apart: 5 -> 0, of which waited for: 5 -> 0; matrix products, arithmetic and copies ran while one was open for 8% -> 0% of each run, Pallas kernels for 0% -> 0%
where the time goes in v1:
time: 123 us
  Pallas kernels  114 us (93%)
  local copies, waits for them, and re-layouts  7.4 us (6%)
  between operations  1.3 us (1%)
    pallas_call x1, Pallas kernels, body(): pl.pallas_call(functools.partial(mesa_kernel, (nx, nz, ny, heads, tokens,...  114 us
    unnamed x9, local copies, waits for them, and re-layouts  7.4 us

profile of v1, /device:TPU:0, one launch (start us, length us, event | category | flops | bytes accessed | tf_op | source)
XLA Modules:
  0.0 123.1 jit_solution(17662216216173087732)
XLA Ops:
  1.3 1.5 %copy.12.gates_ref = f32[1,256,8]{2,1,0:T(8,128)} copy(f32[1,256,8]{1,2,0:T(8,128)} %param.10) | data formatting | bytes 16384 | tf_op args[2]
  2.8 114.4 %mesa_backward.1 = (bf16[1,256,2048]{2,1,0:T(8,128)(2,1)}, f32[1,256,1024]{2,1,0:T(8,128)}, f32[16,1024]{1,0:T(8,128)}, f32[16,1024]{1,0:T(8,128)}) custom-call(bf16[1,256,2048]{2,1,0:T(8,128)(2,1)} %x_ref.1, bf16[1,256,1024]{2,1,0:T(8,128)(2,1)} %q_ref.1, f32[1,256,8]{2,1,0:T(8,128)} %copy.12.gates_ref, f32[8]{0:T(128)} %reg_ref.1, ...), custom_call_target="tpu_custom_call" | custom-call | tf_op jit(solution)/shard_map/mesa_backward/pallas_call | solution.py:478
  117.2 0.0 copy-start.1
  117.2 0.0 copy-start
  117.2 2.3 %copy.18 = bf16[1,256,2048]{2,1,0:T(8,128)(2,1)} copy(bf16[1,256,2048]{2,1,0:T(8,128)(2,1)} %get-tuple-element.8) | data formatting | bytes 2097152
  119.5 2.3 %copy.19 = f32[1,256,1024]{2,1,0:T(8,128)} copy(f32[1,256,1024]{2,1,0:T(8,128)} %get-tuple-element.9) | data formatting | bytes 2097152
  121.8 0.0 copy-done.1
  121.8 0.6 copy.20
  122.5 0.0 copy-done
  122.5 0.6 copy.21
Async XLA Ops:
  117.2 4.7 %copy-start.1 = (f32[16,1024]{1,0:T(8,128)S(1)}, f32[16,1024]{1,0:T(8,128)}, u32[]{:S(2)}) copy-start(f32[16,1024]{1,0:T(8,128)} %get-tuple-element.10) | copy-start | bytes 196612
  117.2 5.3 %copy-start = (f32[16,1024]{1,0:T(8,128)S(1)}, f32[16,1024]{1,0:T(8,128)}, u32[]{:S(2)}) copy-start(f32[16,1024]{1,0:T(8,128)} %get-tuple-element.11) | copy-start | bytes 196612

commit v2 on v1

--- a/solution.py
+++ b/solution.py
@@ -39,21 +39,45 @@
     return dot(left3(a), right3(b))
 
 
+def pack(sym):
+    half = DK // 2
+    row = lax.broadcasted_iota(jnp.int32, (half, DK), 0)
+    lane = lax.broadcasted_iota(jnp.int32, (half, DK), 1)
+    low = pltpu.roll(sym[half:], half, 1)
+    diag = jnp.sum(jnp.where(lane == row, low, 0.0), axis=0, keepdims=True)
+    return jnp.where(lane < row, low, sym[0:half]), diag
+
+
+def unpack(packed, diag):
+    half = DK // 2
+    row = lax.broadcasted_iota(jnp.int32, (half, DK), 0)
+    lane = lax.broadcasted_iota(jnp.int32, (half, DK), 1)
+    diag = pltpu.roll(jnp.broadcast_to(diag, (half, DK)), half, 1)
+    upper = jnp.where(lane > row, packed, 0.0)
+    lower = pltpu.roll(jnp.where(lane < row, packed, 0.0), half, 1)
+    off = jnp.concatenate([upper, lower], axis=0)
+    on = jnp.concatenate(
+        [jnp.where(lane == row, packed, 0.0), jnp.where(lane == row + half, diag, 0.0)], axis=0
+    )
+    return off + off.T + on
+
+
 def mesa_kernel(
     sizes,
     x_ref, q_ref, gates_ref, reg_ref, wk_ref, wv_ref, g_ref, len_ref,
     ig_ref, qg_ref, kwg_ref, vwg_ref,
-    x_s, w_s, q_s, g_s, gate_s, run_s, tot_s, sw_s, ew_s, fac_snd, fac_rcv,
+    x_s, w_s, q_s, g_s, run_s, tot_s, sw_s, ew_s, fac_snd, fac_rcv,
     kv_s, kt_s, dt_s, vs_s, rhs_s, ewc_s, loc_s,
-    snd1, rcv1, rcv2, snd3, rcv3, rcv4,
+    snd1, rcv1, rcv2, snd3, rcv3, rcv4, tot_snd, tot_rcv, carry_s,
     xs_snd, xs_rcv, xt_s, gr_s, sib_snd, sib_rcv, wp_s,
-    ra1, ra2, ra3, rb1, rb2, rb3, rc1, rc2, rc3,
-    ld_sem, w_sem, fac_sem, x_sem, sib_sem, s1, r1, s2, r2, s3, r3, s4, r4, rs_snd, rs_rcv,
+    ra0, ra1, ra2, ra3, rb0, rb1, rb2, rb3, rc0, rc1, rc2, rc3,
+    ld_sem, w_sem, fac_sem, x_sem, sib_sem, s1, r1, s2, r2, s3, r3, s4, r4, ts, tr, rs_snd, rs_rcv,
 ):
     nx, nz, ny, heads, tokens, width = sizes
     nctx = nz * ny
     groups = heads // PAIR
-    srows = DK // nctx
+    per = 24 // ny
+    gram_rows, pair_rows = DK // 2 // ny, DK // ny
     xb = width // (2 * nx)
     rows = xb // nctx
     half = rows // 2
@@ -82,9 +106,7 @@
         pltpu.make_async_copy(q_ref.at[0, :, cols], q_s.at[h], ld_sem.at[2]).start()
 
     length = len_ref[0, 0]
-    gate_s[...] = jnp.ones_like(gate_s)
-    gate_s[:, 0:heads] = gates_ref[0]
-    run = jnp.log(gate_s[...].T[0:heads])
+    run = jnp.log(gates_ref[0])
     lane = lax.broadcasted_iota(jnp.int32, (heads, tokens), 1)
     step = 1
     while step < tokens:
@@ -95,28 +117,64 @@
     tot_s[...] = total
     sw_s[...] = jnp.exp(run)
     ew_s[...] = jnp.exp(total - run)
-    fac_snd[...] = jnp.exp(total)
+    fac_snd[...] = jnp.exp(total[:, 0:DK])
 
     mask_rows = (lax.broadcasted_iota(jnp.int32, (tokens, 2 * DK), 0) < length).astype(F32)
     mask_lane = (lax.broadcasted_iota(jnp.int32, (1, tokens), 1) < length).astype(F32)
 
-    def all_to_all(src, dst, g, send, recv):
-        for o in range(1, nctx):
-            to = lax.rem(ctx + o, nctx)
+    def across_y(src, dst, g, send, recv):
+        for o in range(1, ny):
+            to = lax.rem(my + o, ny)
             pltpu.make_async_remote_copy(
-                src_ref=src.at[g, to], dst_ref=dst.at[g, ctx], send_sem=send.at[g], recv_sem=recv.at[g],
-                device_id=(dp, to), device_id_type=MESH,
+                src_ref=src.at[g, to], dst_ref=dst.at[g, my], send_sem=send.at[g], recv_sem=recv.at[g],
+                device_id=(dp, mz * ny + to), device_id_type=MESH,
             ).start()
-        pltpu.make_async_copy(src.at[g, ctx], dst.at[g, ctx], recv.at[g]).start()
+        pltpu.make_async_copy(src.at[g, my], dst.at[g, my], recv.at[g]).start()
 
     def wait_all(buf, sem):
         pltpu.make_async_copy(buf, buf, sem).wait()
 
     def wait_sent(buf, g, sem):
-        part = buf.at[g, pl.ds(0, nctx - 1)]
+        part = buf.at[g, pl.ds(0, ny - 1)]
         pltpu.make_async_copy(part, part, sem.at[g]).wait()
 
+    def store_state(buf, g, grams, pairs):
+        head = lax.broadcasted_iota(jnp.int32, (heads, DK), 0)
+        diags = jnp.zeros((heads, DK), F32)
+        for i in range(PAIR):
+            packed, diag = pack(grams[i])
+            diags = jnp.where(head == g * PAIR + i, diag, diags)
+            for to in range(ny):
+                buf[g, to, i * per : i * per + per // 3] = packed[
+                    to * gram_rows : (to + 1) * gram_rows
+                ].reshape(per // 3, 8, DK)
+                buf[g, to, i * per + per // 3 : (i + 1) * per] = pairs[i][
+                    to * pair_rows : (to + 1) * pair_rows
+                ].reshape(2 * per // 3, 8, DK)
+        for to in range(ny):
+            buf[g, to, PAIR * per] = diags
+
+    def load_state(buf, g, i):
+        head = lax.broadcasted_iota(jnp.int32, (heads, DK), 0)
+        diag = jnp.sum(jnp.where(head == g * PAIR + i, buf[g, 0, PAIR * per], 0.0), axis=0, keepdims=True)
+        packed = jnp.concatenate(
+            [buf[g, at, i * per : i * per + per // 3].reshape(gram_rows, DK) for at in range(ny)], axis=0
+        )
+        pair = jnp.concatenate(
+            [buf[g, at, i * per + per // 3 : (i + 1) * per].reshape(pair_rows, DK) for at in range(ny)],
+            axis=0,
+        )
+        return unpack(packed, diag), pair
+
+    def factors(c, g):
+        return [fac_rcv[c, pl.ds(g * PAIR + i, 1), :] for i in range(PAIR)] + [fac_rcv[c]]
+
+    def decayed(factor, tiles):
+        scaled = [tiles[i * per : (i + 1) * per] * factor[i] for i in range(PAIR)]
+        return jnp.concatenate(scaled + [tiles[PAIR * per :] * factor[PAIR]], axis=0)
+
     def project(g):
+        grams, pairs = [], []
         for i in range(PAIR):
             h = g * PAIR + i
             wait_all(w_s.at[h], w_sem.at[h])
@@ -126,7 +184,9 @@
             kt = kv[:, 0:DK].T
             kt_s[h, 0], kt_s[h, 1] = split(kt)
             state = dot3(split(kt * ew_s[pl.ds(h, 1), :]), parts)
-            snd1[g, :, i] = state.reshape(nctx, srows, 2 * DK)
+            grams.append(state[:, 0:DK])
+            pairs.append(state[:, DK:])
+        store_state(snd1, g, grams, pairs)
 
     def tables(g):
         for i in range(PAIR):
@@ -146,22 +206,56 @@
             vs_s[h] = scores
             rhs_s[h] = dot3((kt_s[h, 0], kt_s[h, 1]), split(scores))
 
-    def prefix(buf, g, order):
-        held = [jnp.zeros((srows, 2 * DK), F32) for _ in range(PAIR)]
-        for c in order:
-            for i in range(PAIR):
-                mine = buf[g, c, i]
-                buf[g, c, i] = held[i]
-                held[i] = fac_rcv[c, pl.ds(g * PAIR + i, 1), :] * held[i] + mine
-
-    def solve(g):
-        state = [rcv2[g, :, i].reshape(DK, 2 * DK) for i in range(PAIR)]
+    def prefix_y(buf, g, back):
+        held = None
+        for at in reversed(range(ny)) if back else range(ny):
+            mine = buf[g, at]
+            if held is None:
+                buf[g, at] = jnp.zeros_like(mine)
+                held = mine
+            else:
+                buf[g, at] = held
+                held = decayed(factors(mz * ny + at, g), held) + mine
+        tot_snd[back, g] = held
+        for o in range(1, nz):
+            to = lax.rem(mz + o, nz)
+
+            @pl.when(to < mz if back else to > mz)
+            def _():
+                total_copy(back, g, to).start()
+
+    def total_copy(back, g, to):
+        return pltpu.make_async_remote_copy(
+            src_ref=tot_snd.at[back, g], dst_ref=tot_rcv.at[back, g, mz],
+            send_sem=ts.at[back, g, to], recv_sem=tr.at[back, g, mz],
+            device_id=(dp, to * ny + my), device_id_type=MESH,
+        )
+
+    def prefix_z(buf, g, back):
+        carry_s[...] = jnp.zeros_like(carry_s)
+        for at in reversed(range(nz)) if back else range(nz):
+
+            @pl.when(at > mz if back else at < mz)
+            def _():
+                wait_all(tot_rcv.at[back, g, at], tr.at[back, g, at])
+                factor = factors(at * ny, g)
+                for y in range(1, ny):
+                    factor = [a * b for a, b in zip(factor, factors(at * ny + y, g))]
+                carry_s[...] = decayed(factor, carry_s[...]) + tot_rcv[back, g, at]
+
+        carried = carry_s[...]
+        for at in reversed(range(ny)) if back else range(ny):
+            buf[g, at] = buf[g, at] + carried
+            carried = decayed(factors(mz * ny + at, g), carried)
+
+    def solve(g, between):
+        state = [load_state(rcv2, g, i) for i in range(PAIR)]
         x, r, p, rr, keys, kts, big, gts = ([None] * PAIR for _ in range(8))
         for i in range(PAIR):
             h = g * PAIR + i
             qt = q_s[h].astype(F32).T
             gts[i] = ((g_s[h].astype(F32)).T * mask_lane).astype(BF16)
-            gram, pair = split(state[i][:, 0:DK]), split(state[i][:, DK:])
+            gram, pair = split(state[i][0]), split(state[i][1])
             right = rhs_s[h] + sw_s[pl.ds(h, 1), :] * dot(
                 jnp.concatenate(pair, axis=1), jnp.concatenate([gts[i], gts[i]], axis=0)
             )
@@ -190,6 +284,8 @@
                     following = jnp.sum(r[i] * r[i], axis=0, keepdims=True)
                     p[i] = r[i] + (following / (rr[i] + TINY)) * p[i]
                     rr[i] = following
+            between[it]()
+        grams, pairs = [], []
         for i in range(PAIR):
             h = g * PAIR + i
             xt, yt = x[i][:, 0:tokens], x[i][:, tokens:]
@@ -202,20 +298,21 @@
                 jnp.concatenate([y_low, jnp.zeros_like(gn)], axis=1),
             )
             back = dot3(split(xt * sw_s[pl.ds(h, 1), :]), yg)
-            snd3[g, :, i] = back.reshape(nctx, srows, 2 * DK)
+            grams.append(-(back[:, 0:DK] + back[:, 0:DK].T))
+            pairs.append(back[:, DK:])
             table = jnp.concatenate([dt_s[h]] * 2, axis=1)
             scores = dot3(keys[i], split(x[i])) * table
             sol, adj = scores[:, 0:tokens], scores[:, tokens:]
             from_x = dot3(split(vs_s[h] - adj), split(xn))
             from_yg = dot3(split(sol), yg)
             loc_s[h] = jnp.concatenate([from_x - from_yg[:, 0:DK], from_yg[:, DK:]], axis=1)
+        store_state(snd3, g, grams, pairs)
 
     def gradients(g):
         for i in range(PAIR):
             h = g * PAIR + i
-            state = rcv4[g, :, i].reshape(DK, 2 * DK)
-            cross, pair_t = state[:, 0:DK], state[:, DK:]
-            sym, pair = -(cross + cross.T), pair_t.T
+            sym, pair_t = load_state(rcv4, g, i)
+            pair = pair_t.T
             both = jnp.concatenate(
                 [
                     jnp.concatenate([sym, pair_t], axis=1),
@@ -237,45 +334,80 @@
 
     me = {"x": mx, "z": mz, "y": my}
     count = {"x": nx, "z": nz, "y": ny}
-    lanes3, lanes1 = pl.ds(0, 3 * DK), pl.ds(3 * DK, DK)
-    parts = (
-        ("xyz", pl.ds(0, half), lanes3, (ra1, ra2, ra3)),
-        ("yzx", pl.ds(half, half), lanes3, (rb1, rb2, rb3)),
-        ("zxy", pl.ds(0, rows), lanes1, (rc1, rc2, rc3)),
-    )
+    parts = [
+        (order, rws, lns, bufs)
+        for (order, rws, lns), bufs in zip(
+            scatter_parts(rows), ((ra0, ra1, ra2, ra3), (rb0, rb1, rb2, rb3), (rc0, rc1, rc2, rc3))
+        )
+    ]
 
     def device(axis, at):
         place = dict(me)
         place[axis] = at
         return (place["x"] * 2 + mc, place["z"] * ny + place["y"])
 
-    def chunk(n, part, g, at):
+    def chunk(n, part, g, at, side=None):
         order, rws, lns, bufs = parts[part]
         left = [a for a in "xzy" if a not in order[:n]]
         spot = tuple(at if a == order[n] else slice(None) for a in left)
+        if side is not None:
+            cut = halved(order, count)
+            spot = tuple(
+                pl.ds(side * (count[a] // 2), count[a] // 2) if a == cut else b for a, b in zip(left, spot)
+            )
         if n == 0:
             return wp_s.at[(g,) + spot + (rws, lns)]
-        return bufs[n - 1].at[(g, 0) + spot]
+        return bufs[n].at[(g, 0) + spot]
+
+    def send(src, dst, part, n, g, axis, to):
+        pltpu.make_async_remote_copy(
+            src_ref=src, dst_ref=dst, send_sem=rs_snd.at[part, n, g], recv_sem=rs_rcv.at[part, n, g],
+            device_id=device(axis, to), device_id_type=MESH,
+        ).start()
+
+    def sides(axis):
+        return lax.rem(me[axis] + 1, count[axis]), lax.rem(me[axis] + count[axis] - 1, count[axis])
+
+    def scatter_far(g):
+        for part, (order, rws, lns, bufs) in enumerate(parts):
+            axis = order[0]
+            if count[axis] == 4:
+                for side, to in enumerate(sides(axis)):
+                    far = lax.rem(me[axis] + 2, 4)
+                    send(chunk(0, part, g, far, side), bufs[0].at[g, side], part, 0, g, axis, to)
+
+    def scatter_near(g):
+        for part, (order, rws, lns, bufs) in enumerate(parts):
+            axis = order[0]
+            if count[axis] == 4:
+                wait_all(bufs[0].at[g], rs_rcv.at[part, 0, g])
+                for side, to in enumerate(sides(axis)):
+                    half_ref = chunk(0, part, g, to, side)
+                    half_ref[...] = half_ref[...] + bufs[0][g, side]
+                    send(chunk(0, part, g, to), bufs[1].at[g, side], part, 1, g, axis, to)
+            else:
+                scatter_direct(0, part, g)
+
+    def scatter_direct(n, part, g):
+        order, rws, lns, bufs = parts[part]
+        axis = order[n]
+        for o in range(1, count[axis]):
+            to = lax.rem(me[axis] + o, count[axis])
+            send(chunk(n, part, g, to), bufs[n + 1].at[g, o - 1], part, n + 1, g, axis, to)
 
     def scatter_start(n, g):
-        for part, (order, rws, lns, bufs) in enumerate(parts):
-            axis = order[n]
-            for o in range(1, count[axis]):
-                to = lax.rem(me[axis] + o, count[axis])
-                pltpu.make_async_remote_copy(
-                    src_ref=chunk(n, part, g, to), dst_ref=bufs[n].at[g, o - 1],
-                    send_sem=rs_snd.at[part, n, g], recv_sem=rs_rcv.at[part, n, g],
-                    device_id=device(axis, to), device_id_type=MESH,
-                ).start()
+        for part in range(3):
+            scatter_direct(n, part, g)
 
     def scatter_add(n, g):
         for part, (order, rws, lns, bufs) in enumerate(parts):
-            wait_all(bufs[n].at[g], rs_rcv.at[part, n, g])
             summed = chunk(n, part, g, me[order[n]])[...]
-            for o in range(count[order[n]] - 1):
-                summed = summed + bufs[n][g, o]
+            if count[order[n]] > 1:
+                wait_all(bufs[n + 1].at[g], rs_rcv.at[part, n + 1, g])
+                for o in range(bufs[n + 1].shape[1]):
+                    summed = summed + bufs[n + 1][g, o]
             if n < 2:
-                bufs[n][g, 0] = summed
+                bufs[n + 1][g, 0] = summed
             else:
                 first = pl.ds(pl.multiple_of(g * PAIR * DK, DK), DK)
                 second = pl.ds(pl.multiple_of(g * PAIR * DK + DK, DK), DK)
@@ -292,7 +424,7 @@
         for k in range(nx):
             out = dot(xt_s[k * xb : (k + 1) * xb, :], gr_s[g])
             wp_s[g, k] = out.reshape(nz, ny, rows, PAIR * 2 * DK)
-        scatter_start(0, g)
+        scatter_far(g)
 
     def input_gradient():
         def columns(n, carry):
@@ -319,11 +451,11 @@
             device_id=(dp, to), device_id_type=MESH,
         ).start()
     pltpu.make_async_copy(fac_snd, fac_rcv.at[ctx], fac_sem.at[1]).start()
-    all_to_all(snd1, rcv1, 0, s1, r1)
+    across_y(snd1, rcv1, 0, s1, r1)
 
     def project_next(g, carry):
         project(g)
-        all_to_all(snd1, rcv1, g, s1, r1)
+        across_y(snd1, rcv1, g, s1, r1)
         return carry
 
     lax.fori_loop(1, groups, project_next, 0)
@@ -339,44 +471,48 @@
     wait_all(g_s, ld_sem.at[1])
     wait_all(q_s, ld_sem.at[2])
 
-    def tables_next(g, carry):
-        tables(g)
+    wait_all(fac_rcv, fac_sem.at[1])
+
+    def during(s, first, fn):
+        @pl.when(jnp.logical_and(s >= first, s < first + groups))
+        def _():
+            fn(s - first)
+
+    def forward_y(g):
+        wait_all(rcv1.at[g], r1.at[g])
+        prefix_y(rcv1, g, 0)
+
+    def forward_z(g):
+        prefix_z(rcv1, g, 0)
+        across_y(rcv1, rcv2, g, s2, r2)
+
+    def backward_y(g):
+        wait_all(rcv3.at[g], r3.at[g])
+        prefix_y(rcv3, g, 1)
+
+    def backward_z(g):
+        prefix_z(rcv3, g, 1)
+        across_y(rcv3, rcv4, g, s4, r4)
+
+    def tables_next(s, carry):
+        during(s, 0, tables)
+        during(s, 0, forward_y)
+        during(s, 1, forward_z)
         return carry
 
-    lax.fori_loop(0, groups, tables_next, 0)
+    lax.fori_loop(0, groups + 1, tables_next, 0)
     for k in range(nx):
         mine = pl.ds(pl.multiple_of(k * 2 * xb + mc * xb, xb), xb)
         xt_s[k * xb : (k + 1) * xb, 0:tokens] = x_s[:, mine].astype(F32).T.astype(BF16)
     x_copy.wait_recv()
     for k in range(nx):
         xt_s[k * xb : (k + 1) * xb, tokens:] = xs_rcv[:, k * xb : (k + 1) * xb].T.astype(BF16)
-    wait_all(fac_rcv, fac_sem.at[1])
-
-    def during(s, first, fn):
-        @pl.when(jnp.logical_and(s >= first, s < first + groups))
-        def _():
-            fn(s - first)
-
-    def forward_prefix(g):
-        wait_all(rcv1.at[g], r1.at[g])
-        prefix(rcv1, g, range(nctx))
-        all_to_all(rcv1, rcv2, g, s2, r2)
-
-    def solves(g):
-        wait_all(rcv2.at[g], r2.at[g])
-        solve(g)
-        all_to_all(snd3, rcv3, g, s3, r3)
 
     def backward_grads(g):
         wait_all(rcv4.at[g], r4.at[g])
         gradients(g)
         sib_copy(g).start()
 
-    def backward_prefix(g):
-        wait_all(rcv3.at[g], r3.at[g])
-        prefix(rcv3, g, range(nctx - 1, -1, -1))
-        all_to_all(rcv3, rcv4, g, s4, r4)
-
     def reduce_two(g):
         scatter_add(0, g)
         scatter_start(1, g)
@@ -388,19 +524,45 @@
     def reduce_last(g):
         scatter_add(2, g)
 
-    def one(s, carry):
-        during(s, 0, forward_prefix)
-        during(s, 1, solves)
-        during(s, 3, backward_grads)
-        during(s, 2, backward_prefix)
-        during(s, 3, weight_part)
-        pl.when(s == groups + 3)(input_gradient)
-        during(s, 6, reduce_last)
-        during(s, 5, reduce_three)
-        during(s, 4, reduce_two)
+    def steps(s):
+        def zero():
+            during(s, 3, weight_part)
+
+        def one():
+            during(s, 2, backward_z)
+            during(s, 5, reduce_three)
+
+        def two():
+            during(s, 4, reduce_two)
+
+        def three():
+            during(s, 1, backward_y)
+            during(s, 3, scatter_near)
+
+        def end():
+            during(s, 2, backward_grads)
+            during(s, 6, reduce_last)
+
+        return (zero, one, two, three), end
+
+    def with_solve(s, carry):
+        between, end = steps(s)
+        wait_all(rcv2.at[s], r2.at[s])
+        solve(s, between)
+        across_y(snd3, rcv3, s, s3, r3)
+        end()
         return carry
 
-    lax.fori_loop(0, groups + 6, one, 0)
+    def without_solve(s, carry):
+        between, end = steps(s)
+        for fn in between:
+            fn()
+        pl.when(s == groups + 2)(input_gradient)
+        end()
+        return carry
+
+    lax.fori_loop(0, groups, with_solve, 0)
+    lax.fori_loop(groups, groups + 6, without_solve, 0)
 
     sent = pltpu.make_async_copy(
         fac_rcv.at[pl.ds(0, nctx - 1)], fac_rcv.at[pl.ds(0, nctx - 1)], fac_sem.at[0]
@@ -414,41 +576,61 @@
         wait_sent(snd3, g, s3)
         wait_sent(rcv3, g, s4)
         sib_copy(g).wait_send()
-        for part in range(3):
-            for n in range(3):
-                buf = parts[part][3][n].at[g]
-                wait_all(buf, rs_snd.at[part, n, g])
+        for part, (order, rws, lns, bufs) in enumerate(parts):
+            for n in range(4):
+                if count[order[max(n - 1, 0)]] > 1 and (n > 0 or count[order[0]] == 4):
+                    wait_all(bufs[n].at[g], rs_snd.at[part, n, g])
+        for back in range(2):
+            for o in range(1, nz):
+                to = lax.rem(mz + o, nz)
+
+                @pl.when(to < mz if back else to > mz)
+                def _():
+                    total_copy(back, g, to).wait_send()
+
         return carry
 
     lax.fori_loop(0, groups, drain, 0)
+
+
+def scatter_parts(rows):
+    return (
+        ("xzy", pl.ds(0, rows // 2), pl.ds(0, 3 * DK)),
+        ("zxy", pl.ds(rows // 2, rows // 2), pl.ds(0, 3 * DK)),
+        ("yxz", pl.ds(0, rows), pl.ds(3 * DK, DK)),
+    )
+
+
+def halved(order, count):
+    return [a for a in "xzy" if a != order[0] and count[a] % 2 == 0][0]
 
 
 def solution(mesh):
     nx = mesh.shape["dp"] // 2
     nctx = mesh.shape["ctx"]
-    nz = ny = {16: 4, 4: 2}[nctx]
+    ny = min(nctx, 4)
+    nz = nctx // ny
 
     def body(layer_input, queries, gates, regularizer, key_weight, value_weight, out_cotangent, lengths):
         tokens, width = layer_input.shape[1:]
         heads = gates.shape[2]
         groups = heads // PAIR
         rows = width // (2 * nx * nctx)
-        srows = DK // nctx
+        tiles = PAIR * 24 // ny + 1
         wide = PAIR * 2 * DK
-        state = lambda: pltpu.VMEM((groups, nctx, PAIR, srows, 2 * DK), F32)
+        state = lambda: pltpu.VMEM((groups, ny, tiles, 8, DK), F32)
         dma = lambda *shape: pltpu.SemaphoreType.DMA(shape)
         scratch = [
             pltpu.VMEM((tokens, width), BF16),
             pltpu.VMEM((heads, width, 2 * DK), BF16),
             pltpu.VMEM((heads, tokens, DK), BF16),
             pltpu.VMEM((heads, tokens, DK), BF16),
-            pltpu.VMEM((tokens, DK), F32),
             pltpu.VMEM((heads, tokens), F32),
             pltpu.VMEM((heads, tokens), F32),
             pltpu.VMEM((heads, tokens), F32),
             pltpu.VMEM((heads, tokens), F32),
-            pltpu.VMEM((heads, 2 * DK), F32),
-            pltpu.VMEM((nctx, heads, 2 * DK), F32),
+            pltpu.VMEM((heads, DK), F32),
+            pltpu.VMEM((nctx, heads, DK), F32),
             pltpu.VMEM((heads, 2, tokens, 2 * DK), BF16),
             pltpu.VMEM((heads, 2, DK, tokens), BF16),
             pltpu.VMEM((heads, tokens, tokens), F32),
@@ -457,6 +639,9 @@
             pltpu.VMEM((heads, tokens, DK), F32),
             pltpu.VMEM((heads, tokens, 2 * DK), F32),
             state(), state(), state(), state(), state(), state(),
+            pltpu.VMEM((2, groups, tiles, 8, DK), F32),
+            pltpu.VMEM((2, groups, nz, tiles, 8, DK), F32),
+            pltpu.VMEM((tiles, 8, DK), F32),
             pltpu.VMEM((tokens, width // 2), F32),
             pltpu.VMEM((tokens, width // 2), F32),
             pltpu.VMEM((width // 2, 2 * tokens), BF16),
@@ -466,12 +651,16 @@
             pltpu.VMEM((groups, nx, nz, ny, rows, wide), F32),
         ]
         count = {"x": nx, "z": nz, "y": ny}
-        for order, rws, lns in (("xyz", rows // 2, 3 * DK), ("yzx", rows // 2, 3 * DK), ("zxy", rows, DK)):
+        for order, rws, lns in scatter_parts(rows):
+            cut = halved(order, count)
+            shape = tuple(count[a] // 2 if a == cut else count[a] for a in "xzy" if a != order[0])
+            scratch.append(pltpu.VMEM((groups, 2) + shape + (rws.size, lns.size), F32))
             for n in range(3):
+                slots = 2 if n == 0 and count[order[0]] == 4 else max(count[order[n]] - 1, 1)
                 left = tuple(count[a] for a in "xzy" if a not in order[: n + 1])
-                scratch.append(pltpu.VMEM((groups, count[order[n]] - 1) + left + (rws, lns), F32))
+                scratch.append(pltpu.VMEM((groups, slots) + left + (rws.size, lns.size), F32))
         scratch += [dma(3), dma(heads), dma(2), dma(2), dma(2, groups)]
-        scratch += [dma(groups)] * 8 + [dma(3, 3, groups)] * 2
+        scratch += [dma(groups)] * 8 + [dma(2, groups, nz)] * 2 + [dma(3, 4, groups)] * 2
         any_space = pl.BlockSpec(memory_space=pl.ANY)
         vmem = pl.BlockSpec(memory_space=pltpu.VMEM)
         smem = pl.BlockSpec(memory_space=pltpu.SMEM)
@@ -490,7 +679,7 @@
                 collective_id=0, has_side_effects=True, vmem_limit_bytes=63 << 20
             ),
             name="mesa_backward",
-        )(layer_input, queries, gates, regularizer, key_weight, value_weight, out_cotangent, lengths)
+        )(layer_input, queries, jnp.swapaxes(gates, 1, 2), regularizer, key_weight, value_weight, out_cotangent, lengths)
 
     in_specs = (
         P("dp", "ctx", None),

time: 123 us -> 113 us (0.919)
  Pallas kernels: 114 us -> 106 us
  local copies, waits for them, and re-layouts: 7.4 us -> 5.91 us
    pallas_call x1, Pallas kernels: 114 us -> 106 us  [body(): pl.pallas_call(functools.partial(mesa_kernel, (nx, nz, ny, heads, tokens,...]
    unnamed x9 -> x8, local copies, waits for them, and re-layouts: 7.4 us -> 5.91 us
where the time goes in v2:
time: 113 us
  Pallas kernels  106 us (94%)
  local copies, waits for them, and re-layouts  5.91 us (5%)
  between operations  1.31 us (1%)
    pallas_call x1, Pallas kernels, body(): pl.pallas_call(functools.partial(mesa_kernel, (nx, nz, ny, heads, tokens,...  106 us
    unnamed x8, local copies, waits for them, and re-layouts  5.91 us

profile of v2, /device:TPU:0, one launch (start us, length us, event | category | flops | bytes accessed | tf_op | source)
XLA Modules:
  0.0 113.1 jit_solution(10174126340463280680)
XLA Ops:
  1.3 105.9 %mesa_backward.1 = (bf16[1,256,2048]{2,1,0:T(8,128)(2,1)}, f32[1,256,1024]{2,1,0:T(8,128)}, f32[16,1024]{1,0:T(8,128)}, f32[16,1024]{1,0:T(8,128)}) custom-call(bf16[1,256,2048]{2,1,0:T(8,128)(2,1)} %x_ref.1, bf16[1,256,1024]{2,1,0:T(8,128)(2,1)} %q_ref.1, f32[1,8,256]{2,1,0:T(8,128)} %bitcast.1, f32[8]{0:T(128)} %reg_ref.1, bf16[2048,1024]{1,0:T(8,128)(2,1)} %wk_ref.1, ...), custom_call_target="tpu_custom_call" | custom-call | tf_op jit(solution)/shard_map/mesa_backward/pallas_call | solution.py:667
  107.2 0.0 copy-start.1
  107.2 0.0 copy-start
  107.2 2.3 %copy.17 = bf16[1,256,2048]{2,1,0:T(8,128)(2,1)} copy(bf16[1,256,2048]{2,1,0:T(8,128)(2,1)} %get-tuple-element.8) | data formatting | bytes 2097152
  109.6 2.3 %copy.18 = f32[1,256,1024]{2,1,0:T(8,128)} copy(f32[1,256,1024]{2,1,0:T(8,128)} %get-tuple-element.9) | data formatting | bytes 2097152
  111.9 0.0 copy-done.1
  111.9 0.6 copy.19
  112.5 0.0 copy-done
  112.5 0.6 copy.20
Async XLA Ops:
  107.2 4.7 %copy-start.1 = (f32[16,1024]{1,0:T(8,128)S(1)}, f32[16,1024]{1,0:T(8,128)}, u32[]{:S(2)}) copy-start(f32[16,1024]{1,0:T(8,128)} %get-tuple-element.10) | copy-start | bytes 196612
  107.2 5.3 %copy-start = (f32[16,1024]{1,0:T(8,128)S(1)}, f32[16,1024]{1,0:T(8,128)}, u32[]{:S(2)}) copy-start(f32[16,1024]{1,0:T(8,128)} %get-tuple-element.11) | copy-start | bytes 196612

commit v3 on v2

--- a/solution.py
+++ b/solution.py
@@ -409,8 +409,7 @@
             if n < 2:
                 bufs[n + 1][g, 0] = summed
             else:
-                first = pl.ds(pl.multiple_of(g * PAIR * DK, DK), DK)
-                second = pl.ds(pl.multiple_of(g * PAIR * DK + DK, DK), DK)
+                first, second = (pl.ds((g * PAIR + i) * DK, DK) for i in range(PAIR))
                 if part < 2:
                     kwg_ref[rws, first] = summed[:, 0:DK]
                     vwg_ref[rws, first] = summed[:, DK : 2 * DK]
@@ -441,6 +440,41 @@
 
         lax.fori_loop(0, width // 256, columns, 0)
 
+    def forward_y(g):
+        wait_all(rcv1.at[g], r1.at[g])
+        prefix_y(rcv1, g, 0)
+
+    def forward_z(g):
+        prefix_z(rcv1, g, 0)
+        across_y(rcv1, rcv2, g, s2, r2)
+
+    def backward_y(g):
+        wait_all(rcv3.at[g], r3.at[g])
+        prefix_y(rcv3, g, 1)
+
+    def backward_z(g):
+        prefix_z(rcv3, g, 1)
+        across_y(rcv3, rcv4, g, s4, r4)
+
+    def backward_grads(g):
+        wait_all(rcv4.at[g], r4.at[g])
+        gradients(g)
+        sib_copy(g).start()
+
+    def reduce_two(g):
+        scatter_add(0, g)
+        scatter_start(1, g)
+
+    def reduce_three(g):
+        scatter_add(1, g)
+        scatter_start(2, g)
+
+    def reduce_last(g):
+        scatter_add(2, g)
+
+    def send_state(g):
+        across_y(snd1, rcv1, g, s1, r1)
+
     wait_all(x_s, ld_sem.at[0])
     project(0)
     pl.semaphore_wait(barrier, nctx - 1 + 1 + nx - 1)
@@ -451,15 +485,20 @@
             device_id=(dp, to), device_id_type=MESH,
         ).start()
     pltpu.make_async_copy(fac_snd, fac_rcv.at[ctx], fac_sem.at[1]).start()
-    across_y(snd1, rcv1, 0, s1, r1)
-
-    def project_next(g, carry):
-        project(g)
-        across_y(snd1, rcv1, g, s1, r1)
-        return carry
-
-    lax.fori_loop(1, groups, project_next, 0)
-
+    send_state(0)
+    project(1)
+    send_state(1)
+    wait_all(g_s, ld_sem.at[1])
+    wait_all(q_s, ld_sem.at[2])
+    tables(0)
+    tables(1)
+    wait_all(fac_rcv, fac_sem.at[1])
+    forward_y(0)
+    project(2)
+    forward_y(1)
+    forward_z(0)
+    send_state(2)
+    forward_z(1)
     for k in range(nx):
         theirs = pl.ds(pl.multiple_of(k * 2 * xb + (1 - mc) * xb, xb), xb)
         xs_snd[:, k * xb : (k + 1) * xb] = x_s[:, theirs].astype(F32)
@@ -468,101 +507,74 @@
         device_id=(sib, ctx), device_id_type=MESH,
     )
     x_copy.start()
-    wait_all(g_s, ld_sem.at[1])
-    wait_all(q_s, ld_sem.at[2])
-
-    wait_all(fac_rcv, fac_sem.at[1])
-
-    def during(s, first, fn):
-        @pl.when(jnp.logical_and(s >= first, s < first + groups))
-        def _():
-            fn(s - first)
-
-    def forward_y(g):
-        wait_all(rcv1.at[g], r1.at[g])
-        prefix_y(rcv1, g, 0)
-
-    def forward_z(g):
-        prefix_z(rcv1, g, 0)
-        across_y(rcv1, rcv2, g, s2, r2)
-
-    def backward_y(g):
-        wait_all(rcv3.at[g], r3.at[g])
-        prefix_y(rcv3, g, 1)
-
-    def backward_z(g):
-        prefix_z(rcv3, g, 1)
-        across_y(rcv3, rcv4, g, s4, r4)
-
-    def tables_next(s, carry):
-        during(s, 0, tables)
-        during(s, 0, forward_y)
-        during(s, 1, forward_z)
-        return carry
-
-    lax.fori_loop(0, groups + 1, tables_next, 0)
+    project(3)
+    send_state(3)
+    tables(2)
+    tables(3)
+    forward_y(2)
     for k in range(nx):
         mine = pl.ds(pl.multiple_of(k * 2 * xb + mc * xb, xb), xb)
         xt_s[k * xb : (k + 1) * xb, 0:tokens] = x_s[:, mine].astype(F32).T.astype(BF16)
-    x_copy.wait_recv()
-    for k in range(nx):
-        xt_s[k * xb : (k + 1) * xb, tokens:] = xs_rcv[:, k * xb : (k + 1) * xb].T.astype(BF16)
-
-    def backward_grads(g):
-        wait_all(rcv4.at[g], r4.at[g])
-        gradients(g)
-        sib_copy(g).start()
-
-    def reduce_two(g):
-        scatter_add(0, g)
-        scatter_start(1, g)
-
-    def reduce_three(g):
-        scatter_add(1, g)
-        scatter_start(2, g)
-
-    def reduce_last(g):
-        scatter_add(2, g)
-
-    def steps(s):
+
+    def during(s, first, fn, count=groups):
+        @pl.when(jnp.logical_and(s >= first, s < first + count))
+        def _():
+            fn(s - first)
+
+    def with_solve(s, carry):
         def zero():
             during(s, 3, weight_part)
+            pl.when(s == 0)(lambda: forward_z(2))
 
         def one():
+            pl.when(s == 0)(lambda: forward_y(3))
             during(s, 2, backward_z)
-            during(s, 5, reduce_three)
 
         def two():
-            during(s, 4, reduce_two)
+            pl.when(s == 0)(lambda: forward_z(3))
 
         def three():
             during(s, 1, backward_y)
             during(s, 3, scatter_near)
 
-        def end():
-            during(s, 2, backward_grads)
-            during(s, 6, reduce_last)
-
-        return (zero, one, two, three), end
-
-    def with_solve(s, carry):
-        between, end = steps(s)
         wait_all(rcv2.at[s], r2.at[s])
-        solve(s, between)
+        solve(s, (zero, one, two, three))
         across_y(snd3, rcv3, s, s3, r3)
-        end()
+        during(s, 2, backward_grads)
+
+        @pl.when(s == 0)
+        def _():
+            x_copy.wait_recv()
+            for k in range(nx):
+                xt_s[k * xb : (k + 1) * xb, tokens:] = xs_rcv[:, k * xb : (k + 1) * xb].T.astype(BF16)
+
         return carry
 
-    def without_solve(s, carry):
-        between, end = steps(s)
-        for fn in between:
-            fn()
-        pl.when(s == groups + 2)(input_gradient)
-        end()
-        return carry
-
     lax.fori_loop(0, groups, with_solve, 0)
-    lax.fori_loop(groups, groups + 6, without_solve, 0)
+    backward_z(2)
+    weight_part(1)
+    backward_y(3)
+    backward_grads(2)
+    scatter_near(1)
+    backward_z(3)
+    weight_part(2)
+    reduce_two(0)
+    backward_grads(3)
+    scatter_near(2)
+    weight_part(3)
+    reduce_two(1)
+    reduce_three(0)
+    input_gradient()
+    scatter_near(3)
+    reduce_two(2)
+    reduce_three(1)
+    reduce_last(0)
+    reduce_two(3)
+    reduce_three(2)
+    reduce_last(1)
+    reduce_three(3)
+    reduce_last(2)
+    reduce_last(3)
 
     sent = pltpu.make_async_copy(
         fac_rcv.at[pl.ds(0, nctx - 1)], fac_rcv.at[pl.ds(0, nctx - 1)], fac_sem.at[0]
@@ -595,9 +607,9 @@
 
 def scatter_parts(rows):
     return (
-        ("xzy", pl.ds(0, rows // 2), pl.ds(0, 3 * DK)),
+        ("xyz", pl.ds(0, rows // 2), pl.ds(0, 3 * DK)),
         ("zxy", pl.ds(rows // 2, rows // 2), pl.ds(0, 3 * DK)),
-        ("yxz", pl.ds(0, rows), pl.ds(3 * DK, DK)),
+        ("yzx", pl.ds(0, rows), pl.ds(3 * DK, DK)),
     )
 
 

time: 113 us -> 114 us (level)
  no operation moved by 1% of the time
where the time goes in v3:
time: 114 us; the launch traced here: 113 us
  Pallas kernels  106 us (93%)
  local copies, waits for them, and re-layouts  5.91 us (5%)
  between operations  1.31 us (1%)
    pallas_call x1, Pallas kernels, body(): pl.pallas_call(functools.partial(mesa_kernel, (nx, nz, ny, heads, tokens,...  106 us
    unnamed x8, local copies, waits for them, and re-layouts  5.91 us

profile of v3, /device:TPU:0, one launch (start us, length us, event | category | flops | bytes accessed | tf_op | source)
XLA Modules:
  0.0 113.4 jit_solution(9375487986969187378)
XLA Ops:
  1.3 106.1 %mesa_backward.1 = (bf16[1,256,2048]{2,1,0:T(8,128)(2,1)}, f32[1,256,1024]{2,1,0:T(8,128)}, f32[16,1024]{1,0:T(8,128)}, f32[16,1024]{1,0:T(8,128)}) custom-call(bf16[1,256,2048]{2,1,0:T(8,128)(2,1)} %x_ref.1, bf16[1,256,1024]{2,1,0:T(8,128)(2,1)} %q_ref.1, f32[1,8,256]{2,1,0:T(8,128)} %bitcast.1, f32[8]{0:T(128)} %reg_ref.1, bf16[2048,1024]{1,0:T(8,128)(2,1)} %wk_ref.1, ...), custom_call_target="tpu_custom_call" | custom-call | tf_op jit(solution)/shard_map/mesa_backward/pallas_call | solution.py:679
  107.4 0.0 copy-start.1
  107.4 0.0 copy-start
  107.4 2.3 %copy.17 = bf16[1,256,2048]{2,1,0:T(8,128)(2,1)} copy(bf16[1,256,2048]{2,1,0:T(8,128)(2,1)} %get-tuple-element.8) | data formatting | bytes 2097152
  109.8 2.3 %copy.18 = f32[1,256,1024]{2,1,0:T(8,128)} copy(f32[1,256,1024]{2,1,0:T(8,128)} %get-tuple-element.9) | data formatting | bytes 2097152
  112.1 0.0 copy-done.1
  112.1 0.6 copy.19
  112.7 0.0 copy-done
  112.7 0.6 copy.20
Async XLA Ops:
  107.4 4.7 %copy-start.1 = (f32[16,1024]{1,0:T(8,128)S(1)}, f32[16,1024]{1,0:T(8,128)}, u32[]{:S(2)}) copy-start(f32[16,1024]{1,0:T(8,128)} %get-tuple-element.10) | copy-start | bytes 196612
  107.4 5.3 %copy-start = (f32[16,1024]{1,0:T(8,128)S(1)}, f32[16,1024]{1,0:T(8,128)}, u32[]{:S(2)}) copy-start(f32[16,1024]{1,0:T(8,128)} %get-tuple-element.11) | copy-start | bytes 196612

commit v4 on v3

--- a/solution.py
+++ b/solution.py
@@ -66,12 +66,12 @@
     sizes,
     x_ref, q_ref, gates_ref, reg_ref, wk_ref, wv_ref, g_ref, len_ref,
     ig_ref, qg_ref, kwg_ref, vwg_ref,
-    x_s, w_s, q_s, g_s, run_s, tot_s, sw_s, ew_s, fac_snd, fac_rcv,
+    x_s, w_s, q_s, g_s, ig_s, qg_s, run_s, tot_s, sw_s, ew_s, fac_snd, fac_rcv,
     kv_s, kt_s, dt_s, vs_s, rhs_s, ewc_s, loc_s,
     snd1, rcv1, rcv2, snd3, rcv3, rcv4, tot_snd, tot_rcv, carry_s,
-    xs_snd, xs_rcv, xt_s, gr_s, sib_snd, sib_rcv, wp_s,
-    ra0, ra1, ra2, ra3, rb0, rb1, rb2, rb3, rc0, rc1, rc2, rc3,
-    ld_sem, w_sem, fac_sem, x_sem, sib_sem, s1, r1, s2, r2, s3, r3, s4, r4, ts, tr, rs_snd, rs_rcv,
+    xs_snd, xs_rcv, xt_s, gr_s, sib_snd, sib_rcv,
+    wa, ra0, ra1, ra2, ra3, wb, rb0, rb1, rb2, rb3, wc, rc0, rc1, rc2, rc3,
+    out_sem, ld_sem, w_sem, fac_sem, x_sem, sib_sem, s1, r1, s2, r2, s3, r3, s4, r4, ts, tr, rs_snd, rs_rcv,
 ):
     nx, nz, ny, heads, tokens, width = sizes
     nctx = nz * ny
@@ -96,10 +96,13 @@
         )
 
     pltpu.make_async_copy(x_ref.at[0], x_s, ld_sem.at[0]).start()
-    for h in range(heads):
+    def load_weights(h):
         cols = pl.ds(h * DK, DK)
         pltpu.make_async_copy(wk_ref.at[:, cols], w_s.at[h, :, pl.ds(0, DK)], w_sem.at[h]).start()
         pltpu.make_async_copy(wv_ref.at[:, cols], w_s.at[h, :, pl.ds(DK, DK)], w_sem.at[h]).start()
+
+    for h in range(heads):
+        load_weights(h)
     for h in range(heads):
         cols = pl.ds(h * DK, DK)
         pltpu.make_async_copy(g_ref.at[0, :, cols], g_s.at[h], ld_sem.at[1]).start()
@@ -129,10 +132,13 @@
                 src_ref=src.at[g, to], dst_ref=dst.at[g, my], send_sem=send.at[g], recv_sem=recv.at[g],
                 device_id=(dp, mz * ny + to), device_id_type=MESH,
             ).start()
-        pltpu.make_async_copy(src.at[g, my], dst.at[g, my], recv.at[g]).start()
+        dst[g, my] = src[g, my]
 
     def wait_all(buf, sem):
         pltpu.make_async_copy(buf, buf, sem).wait()
+
+    def wait_others(buf, g, sem):
+        wait_all(buf.at[g, pl.ds(0, ny - 1)], sem.at[g])
 
     def wait_sent(buf, g, sem):
         part = buf.at[g, pl.ds(0, ny - 1)]
@@ -290,7 +296,7 @@
             h = g * PAIR + i
             xt, yt = x[i][:, 0:tokens], x[i][:, tokens:]
             xn, yn = xt.T, yt.T
-            qg_ref[0, :, pl.ds(pl.multiple_of(h * DK, DK), DK)] = yn
+            qg_s[:, pl.ds(pl.multiple_of(h * DK, DK), DK)] = yn
             gn = (g_s[h].astype(F32) * mask_rows[:, 0:DK]).astype(BF16)
             y_high, y_low = split(yn)
             yg = (
@@ -334,6 +340,7 @@
 
     me = {"x": mx, "z": mz, "y": my}
     count = {"x": nx, "z": nz, "y": ny}
+    whole = (wa, wb, wc)
     parts = [
         (order, rws, lns, bufs)
         for (order, rws, lns), bufs in zip(
@@ -348,15 +355,12 @@
 
     def chunk(n, part, g, at, side=None):
         order, rws, lns, bufs = parts[part]
-        left = [a for a in "xzy" if a not in order[:n]]
-        spot = tuple(at if a == order[n] else slice(None) for a in left)
+        spot = (at,)
         if side is not None:
-            cut = halved(order, count)
-            spot = tuple(
-                pl.ds(side * (count[a] // 2), count[a] // 2) if a == cut else b for a, b in zip(left, spot)
-            )
+            half_count = count[order[1]] // 2
+            spot = (at, pl.ds(side * half_count, half_count))
         if n == 0:
-            return wp_s.at[(g,) + spot + (rws, lns)]
+            return whole[part].at[(g,) + spot]
         return bufs[n].at[(g, 0) + spot]
 
     def send(src, dst, part, n, g, axis, to):
@@ -422,7 +426,14 @@
         gr_s[g, tokens:, :] = sib_rcv[g].astype(BF16)
         for k in range(nx):
             out = dot(xt_s[k * xb : (k + 1) * xb, :], gr_s[g])
-            wp_s[g, k] = out.reshape(nz, ny, rows, PAIR * 2 * DK)
+            out = out.reshape(nz, ny, rows, PAIR * 2 * DK)
+            for part, (order, rws, lns, bufs) in enumerate(parts):
+                for z in range(nz):
+                    for y in range(ny):
+                        place = {"x": k, "z": z, "y": y}
+                        whole[part][(g,) + tuple(place[a] for a in order)] = out[
+                            z, y, rws.start : rws.start + rws.size, lns.start : lns.start + lns.size
+                        ]
         scatter_far(g)
 
     def input_gradient():
@@ -435,13 +446,13 @@
                     grad, w_s[h, span, :], (((1,), (1,)), ((), ())), preferred_element_type=F32
                 )
                 total = term if total is None else total + term
-            ig_ref[0, :, span] = total.astype(BF16)
+            ig_s[:, span] = total.astype(BF16)
             return carry
 
         lax.fori_loop(0, width // 256, columns, 0)
 
     def forward_y(g):
-        wait_all(rcv1.at[g], r1.at[g])
+        wait_others(rcv1, g, r1)
         prefix_y(rcv1, g, 0)
 
     def forward_z(g):
@@ -449,7 +460,7 @@
         across_y(rcv1, rcv2, g, s2, r2)
 
     def backward_y(g):
-        wait_all(rcv3.at[g], r3.at[g])
+        wait_others(rcv3, g, r3)
         prefix_y(rcv3, g, 1)
 
     def backward_z(g):
@@ -457,7 +468,7 @@
         across_y(rcv3, rcv4, g, s4, r4)
 
     def backward_grads(g):
-        wait_all(rcv4.at[g], r4.at[g])
+        wait_others(rcv4, g, r4)
         gradients(g)
         sib_copy(g).start()
 
@@ -478,21 +489,21 @@
     wait_all(x_s, ld_sem.at[0])
     project(0)
     pl.semaphore_wait(barrier, nctx - 1 + 1 + nx - 1)
+    send_state(0)
     for o in range(1, nctx):
         to = lax.rem(ctx + o, nctx)
         pltpu.make_async_remote_copy(
             src_ref=fac_snd, dst_ref=fac_rcv.at[ctx], send_sem=fac_sem.at[0], recv_sem=fac_sem.at[1],
             device_id=(dp, to), device_id_type=MESH,
         ).start()
-    pltpu.make_async_copy(fac_snd, fac_rcv.at[ctx], fac_sem.at[1]).start()
-    send_state(0)
+    fac_rcv[ctx] = fac_snd[...]
     project(1)
     send_state(1)
     wait_all(g_s, ld_sem.at[1])
     wait_all(q_s, ld_sem.at[2])
     tables(0)
     tables(1)
-    wait_all(fac_rcv, fac_sem.at[1])
+    wait_all(fac_rcv.at[pl.ds(0, nctx - 1)], fac_sem.at[1])
     forward_y(0)
     project(2)
     forward_y(1)
@@ -537,7 +548,7 @@
             during(s, 1, backward_y)
             during(s, 3, scatter_near)
 
-        wait_all(rcv2.at[s], r2.at[s])
+        wait_others(rcv2, s, r2)
         solve(s, (zero, one, two, three))
         across_y(snd3, rcv3, s, s3, r3)
         during(s, 2, backward_grads)
@@ -551,6 +562,8 @@
         return carry
 
     lax.fori_loop(0, groups, with_solve, 0)
+    qg_copy = pltpu.make_async_copy(qg_s, qg_ref.at[0], out_sem.at[0])
+    qg_copy.start()
     backward_z(2)
     weight_part(1)
     backward_y(3)
@@ -565,6 +578,8 @@
     reduce_two(1)
     reduce_three(0)
     input_gradient()
+    ig_copy = pltpu.make_async_copy(ig_s, ig_ref.at[0], out_sem.at[1])
+    ig_copy.start()
     scatter_near(3)
     reduce_two(2)
     reduce_three(1)
@@ -576,6 +591,8 @@
     reduce_last(2)
     reduce_last(3)
 
+    qg_copy.wait()
+    ig_copy.wait()
     sent = pltpu.make_async_copy(
         fac_rcv.at[pl.ds(0, nctx - 1)], fac_rcv.at[pl.ds(0, nctx - 1)], fac_sem.at[0]
     )
@@ -605,16 +622,36 @@
     lax.fori_loop(0, groups, drain, 0)
 
 
+def copy_kernel(a, b, c, d, a_out, b_out, c_out, d_out):
+    for src, dst in ((a, a_out), (b, b_out), (c, c_out), (d, d_out)):
+        dst[...] = src[...]
+
+
+def copied(arrays):
+    steps = 2
+    specs = [
+        pl.BlockSpec((1, a.shape[1] // steps, a.shape[2]), lambda i: (0, i, 0))
+        if len(a.shape) == 3
+        else pl.BlockSpec((a.shape[0] // steps, a.shape[1]), lambda i: (i, 0))
+        for a in arrays
+    ]
+    return pl.pallas_call(
+        copy_kernel,
+        out_shape=tuple(jax.ShapeDtypeStruct(a.shape, a.dtype) for a in arrays),
+        grid=(steps,),
+        in_specs=specs,
+        out_specs=tuple(specs),
+        compiler_params=pltpu.CompilerParams(vmem_limit_bytes=62 << 20),
+        name="results",
+    )(*arrays)
+
+
 def scatter_parts(rows):
     return (
         ("xyz", pl.ds(0, rows // 2), pl.ds(0, 3 * DK)),
         ("zxy", pl.ds(rows // 2, rows // 2), pl.ds(0, 3 * DK)),
         ("yzx", pl.ds(0, rows), pl.ds(3 * DK, DK)),
     )
-
-
-def halved(order, count):
-    return [a for a in "xzy" if a != order[0] and count[a] % 2 == 0][0]
 
 
 def solution(mesh):
@@ -637,6 +674,8 @@
             pltpu.VMEM((heads, width, 2 * DK), BF16),
             pltpu.VMEM((heads, tokens, DK), BF16),
             pltpu.VMEM((heads, tokens, DK), BF16),
+            pltpu.VMEM((tokens, width), BF16),
+            pltpu.VMEM((tokens, heads * DK), F32),
             pltpu.VMEM((heads, tokens), F32),
             pltpu.VMEM((heads, tokens), F32),
             pltpu.VMEM((heads, tokens), F32),
@@ -660,23 +699,22 @@
             pltpu.VMEM((groups, 2 * tokens, wide), BF16),
             pltpu.VMEM((groups, tokens, wide), F32),
             pltpu.VMEM((groups, tokens, wide), F32),
-            pltpu.VMEM((groups, nx, nz, ny, rows, wide), F32),
         ]
         count = {"x": nx, "z": nz, "y": ny}
         for order, rws, lns in scatter_parts(rows):
-            cut = halved(order, count)
-            shape = tuple(count[a] // 2 if a == cut else count[a] for a in "xzy" if a != order[0])
-            scratch.append(pltpu.VMEM((groups, 2) + shape + (rws.size, lns.size), F32))
+            a, b, c = (count[axis] for axis in order)
+            scratch.append(pltpu.VMEM((groups, a, b, c, rws.size, lns.size), F32))
+            scratch.append(pltpu.VMEM((groups, 2, max(b // 2, 1), c, rws.size, lns.size), F32))
             for n in range(3):
                 slots = 2 if n == 0 and count[order[0]] == 4 else max(count[order[n]] - 1, 1)
-                left = tuple(count[a] for a in "xzy" if a not in order[: n + 1])
+                left = tuple(count[a] for a in order[n + 1 :])
                 scratch.append(pltpu.VMEM((groups, slots) + left + (rws.size, lns.size), F32))
-        scratch += [dma(3), dma(heads), dma(2), dma(2), dma(2, groups)]
+        scratch += [dma(2), dma(3), dma(heads), dma(2), dma(2), dma(2, groups)]
         scratch += [dma(groups)] * 8 + [dma(2, groups, nz)] * 2 + [dma(3, 4, groups)] * 2
         any_space = pl.BlockSpec(memory_space=pl.ANY)
         vmem = pl.BlockSpec(memory_space=pltpu.VMEM)
         smem = pl.BlockSpec(memory_space=pltpu.SMEM)
-        return pl.pallas_call(
+        results = pl.pallas_call(
             functools.partial(mesa_kernel, (nx, nz, ny, heads, tokens, width)),
             out_shape=(
                 jax.ShapeDtypeStruct((1, tokens, width), BF16),
@@ -685,13 +723,14 @@
                 jax.ShapeDtypeStruct((rows, heads * DK), F32),
             ),
             in_specs=[any_space, any_space, vmem, smem, any_space, any_space, any_space, smem],
-            out_specs=(vmem, vmem, vmem, vmem),
+            out_specs=(any_space, any_space, vmem, vmem),
             scratch_shapes=scratch,
             compiler_params=pltpu.CompilerParams(
                 collective_id=0, has_side_effects=True, vmem_limit_bytes=63 << 20
             ),
             name="mesa_backward",
         )(layer_input, queries, jnp.swapaxes(gates, 1, 2), regularizer, key_weight, value_weight, out_cotangent, lengths)
+        return copied(results)
 
     in_specs = (
         P("dp", "ctx", None),

time: 114 us -> 113 us (level)
  local copies, waits for them, and re-layouts: 5.91 us -> 0 us
  Pallas kernels: 106 us -> 111 us
    unnamed x8 -> x0, local copies, waits for them, and re-layouts: 5.91 us -> none
    pallas_call x1, Pallas kernels: 106 us -> 109 us  [body(): pl.pallas_call(functools.partial(mesa_kernel, (nx, nz, ny, heads, tokens,...]
    pallas_call x0 -> x1, Pallas kernels: none -> 2.64 us  [copied(): pl.pallas_call(copy_kernel, out_shape=tuple((jax.ShapeDtypeStruct(a.shape...]
where the time goes in v4:
time: 113 us
  Pallas kernels  111 us (98%)
  between operations  1.46 us (1%)
    pallas_call x1, Pallas kernels, body(): pl.pallas_call(functools.partial(mesa_kernel, (nx, nz, ny, heads, tokens,...  109 us
    pallas_call x1, Pallas kernels, copied(): pl.pallas_call(copy_kernel, out_shape=tuple((jax.ShapeDtypeStruct(a.shape...  2.64 us

profile of v4, /device:TPU:0, one launch (start us, length us, event | category | flops | bytes accessed | tf_op | source)
XLA Modules:
  0.0 112.9 jit_solution(15761010515256607837)
XLA Ops:
  1.3 108.8 %mesa_backward.1 = (bf16[1,256,2048]{2,1,0:T(8,128)(2,1)}, f32[1,256,1024]{2,1,0:T(8,128)}, f32[16,1024]{1,0:T(8,128)}, f32[16,1024]{1,0:T(8,128)}) custom-call(bf16[1,256,2048]{2,1,0:T(8,128)(2,1)} %x_ref.1, bf16[1,256,1024]{2,1,0:T(8,128)(2,1)} %q_ref.1, f32[1,8,256]{2,1,0:T(8,128)} %bitcast.1, f32[8]{0:T(128)} %reg_ref.1, bf16[2048,1024]{1,0:T(8,128)(2,1)} %wk_ref.1, ...), custom_call_target="tpu_custom_call" | custom-call | tf_op jit(solution)/shard_map/mesa_backward/pallas_call | solution.py:717
  110.1 2.6 %results.1 = (bf16[1,256,2048]{2,1,0:T(8,128)(2,1)}, f32[1,256,1024]{2,1,0:T(8,128)}, f32[16,1024]{1,0:T(8,128)}, f32[16,1024]{1,0:T(8,128)}) custom-call(bf16[1,256,2048]{2,1,0:T(8,128)(2,1)} %get-tuple-element.8.a, f32[1,256,1024]{2,1,0:T(8,128)} %get-tuple-element.9.b, f32[16,1024]{1,0:T(8,128)} %get-tuple-element.10.c, f32[16,1024]{1,0:T(8,128)} %get-tuple-element.11.d), custom_call_target="tpu_custom_call" | custom-call | tf_op jit(solution)/shard_map/results/pallas_call | solution.py:638

commit v5 on v4

--- a/solution.py
+++ b/solution.py
@@ -126,7 +126,7 @@
     mask_lane = (lax.broadcasted_iota(jnp.int32, (1, tokens), 1) < length).astype(F32)
 
     def across_y(src, dst, g, send, recv):
-        for o in range(1, ny):
+        for o in sorted(range(1, ny), key=lambda o: -min(o, ny - o)):
             to = lax.rem(my + o, ny)
             pltpu.make_async_remote_copy(
                 src_ref=src.at[g, to], dst_ref=dst.at[g, my], send_sem=send.at[g], recv_sem=recv.at[g],
@@ -291,7 +291,7 @@
                     p[i] = r[i] + (following / (rr[i] + TINY)) * p[i]
                     rr[i] = following
             between[it]()
-        grams, pairs = [], []
+        grams, pairs, xns, ygs = [], [], [], []
         for i in range(PAIR):
             h = g * PAIR + i
             xt, yt = x[i][:, 0:tokens], x[i][:, tokens:]
@@ -306,13 +306,18 @@
             back = dot3(split(xt * sw_s[pl.ds(h, 1), :]), yg)
             grams.append(-(back[:, 0:DK] + back[:, 0:DK].T))
             pairs.append(back[:, DK:])
+            xns.append(xn)
+            ygs.append(yg)
+        store_state(snd3, g, grams, pairs)
+        across_y(snd3, rcv3, g, s3, r3)
+        for i in range(PAIR):
+            h = g * PAIR + i
             table = jnp.concatenate([dt_s[h]] * 2, axis=1)
             scores = dot3(keys[i], split(x[i])) * table
             sol, adj = scores[:, 0:tokens], scores[:, tokens:]
-            from_x = dot3(split(vs_s[h] - adj), split(xn))
-            from_yg = dot3(split(sol), yg)
+            from_x = dot3(split(vs_s[h] - adj), split(xns[i]))
+            from_yg = dot3(split(sol), ygs[i])
             loc_s[h] = jnp.concatenate([from_x - from_yg[:, 0:DK], from_yg[:, DK:]], axis=1)
-        store_state(snd3, g, grams, pairs)
 
     def gradients(g):
         for i in range(PAIR):
@@ -522,7 +527,6 @@
     send_state(3)
     tables(2)
     tables(3)
-    forward_y(2)
     for k in range(nx):
         mine = pl.ds(pl.multiple_of(k * 2 * xb + mc * xb, xb), xb)
         xt_s[k * xb : (k + 1) * xb, 0:tokens] = x_s[:, mine].astype(F32).T.astype(BF16)
@@ -535,22 +539,22 @@
     def with_solve(s, carry):
         def zero():
             during(s, 3, weight_part)
-            pl.when(s == 0)(lambda: forward_z(2))
+            pl.when(s == 0)(lambda: forward_y(2))
 
         def one():
             pl.when(s == 0)(lambda: forward_y(3))
             during(s, 2, backward_z)
 
         def two():
+            pl.when(s == 0)(lambda: forward_z(2))
+
+        def three():
             pl.when(s == 0)(lambda: forward_z(3))
-
-        def three():
             during(s, 1, backward_y)
             during(s, 3, scatter_near)
 
         wait_others(rcv2, s, r2)
         solve(s, (zero, one, two, three))
-        across_y(snd3, rcv3, s, s3, r3)
         during(s, 2, backward_grads)
 
         @pl.when(s == 0)

time: 113 us -> 109 us (0.965)
  Pallas kernels: 111 us -> 107 us
    pallas_call x1, Pallas kernels: 109 us -> 105 us  [body(): pl.pallas_call(functools.partial(mesa_kernel, (nx, nz, ny, heads, tokens,...]
where the time goes in v5:
time: 109 us
  Pallas kernels  107 us (98%)
  between operations  1.46 us (1%)
    pallas_call x1, Pallas kernels, body(): pl.pallas_call(functools.partial(mesa_kernel, (nx, nz, ny, heads, tokens,...  105 us
    pallas_call x1, Pallas kernels, copied(): pl.pallas_call(copy_kernel, out_shape=tuple((jax.ShapeDtypeStruct(a.shape...  2.64 us

profile of v5, /device:TPU:0, one launch (start us, length us, event | category | flops | bytes accessed | tf_op | source)
XLA Modules:
  0.0 108.8 jit_solution(72993189534443247)
XLA Ops:
  1.3 104.7 %mesa_backward.1 = (bf16[1,256,2048]{2,1,0:T(8,128)(2,1)}, f32[1,256,1024]{2,1,0:T(8,128)}, f32[16,1024]{1,0:T(8,128)}, f32[16,1024]{1,0:T(8,128)}) custom-call(bf16[1,256,2048]{2,1,0:T(8,128)(2,1)} %x_ref.1, bf16[1,256,1024]{2,1,0:T(8,128)(2,1)} %q_ref.1, f32[1,8,256]{2,1,0:T(8,128)} %bitcast.1, f32[8]{0:T(128)} %reg_ref.1, bf16[2048,1024]{1,0:T(8,128)(2,1)} %wk_ref.1, ...), custom_call_target="tpu_custom_call" | custom-call | tf_op jit(solution)/shard_map/mesa_backward/pallas_call | solution.py:721
  106.0 2.6 %results.1 = (bf16[1,256,2048]{2,1,0:T(8,128)(2,1)}, f32[1,256,1024]{2,1,0:T(8,128)}, f32[16,1024]{1,0:T(8,128)}, f32[16,1024]{1,0:T(8,128)}) custom-call(bf16[1,256,2048]{2,1,0:T(8,128)(2,1)} %get-tuple-element.8.a, f32[1,256,1024]{2,1,0:T(8,128)} %get-tuple-element.9.b, f32[16,1024]{1,0:T(8,128)} %get-tuple-element.10.c, f32[16,1024]{1,0:T(8,128)} %get-tuple-element.11.d), custom_call_target="tpu_custom_call" | custom-call | tf_op jit(solution)/shard_map/results/pallas_call | solution.py:642

commit v6 on v5

--- a/solution.py
+++ b/solution.py
@@ -538,19 +538,19 @@
 
     def with_solve(s, carry):
         def zero():
+            during(s, 2, backward_z)
             during(s, 3, weight_part)
             pl.when(s == 0)(lambda: forward_y(2))
 
         def one():
             pl.when(s == 0)(lambda: forward_y(3))
-            during(s, 2, backward_z)
 
         def two():
             pl.when(s == 0)(lambda: forward_z(2))
+            during(s, 1, backward_y)
 
         def three():
             pl.when(s == 0)(lambda: forward_z(3))
-            during(s, 1, backward_y)
             during(s, 3, scatter_near)
 
         wait_others(rcv2, s, r2)

time: 109 us -> 109 us (level)
  no operation moved by 1% of the time
where the time goes in v6:
time: 109 us
  Pallas kernels  107 us (98%)
  between operations  1.46 us (1%)
    pallas_call x1, Pallas kernels, body(): pl.pallas_call(functools.partial(mesa_kernel, (nx, nz, ny, heads, tokens,...  105 us
    pallas_call x1, Pallas kernels, copied(): pl.pallas_call(copy_kernel, out_shape=tuple((jax.ShapeDtypeStruct(a.shape...  2.64 us

profile of v6, /device:TPU:0, one launch (start us, length us, event | category | flops | bytes accessed | tf_op | source)
XLA Modules:
  0.0 108.7 jit_solution(1284877423512166048)
XLA Ops:
  1.3 104.6 %mesa_backward.1 = (bf16[1,256,2048]{2,1,0:T(8,128)(2,1)}, f32[1,256,1024]{2,1,0:T(8,128)}, f32[16,1024]{1,0:T(8,128)}, f32[16,1024]{1,0:T(8,128)}) custom-call(bf16[1,256,2048]{2,1,0:T(8,128)(2,1)} %x_ref.1, bf16[1,256,1024]{2,1,0:T(8,128)(2,1)} %q_ref.1, f32[1,8,256]{2,1,0:T(8,128)} %bitcast.1, f32[8]{0:T(128)} %reg_ref.1, bf16[2048,1024]{1,0:T(8,128)(2,1)} %wk_ref.1, ...), custom_call_target="tpu_custom_call" | custom-call | tf_op jit(solution)/shard_map/mesa_backward/pallas_call | solution.py:721
  105.8 2.6 %results.1 = (bf16[1,256,2048]{2,1,0:T(8,128)(2,1)}, f32[1,256,1024]{2,1,0:T(8,128)}, f32[16,1024]{1,0:T(8,128)}, f32[16,1024]{1,0:T(8,128)}) custom-call(bf16[1,256,2048]{2,1,0:T(8,128)(2,1)} %get-tuple-element.8.a, f32[1,256,1024]{2,1,0:T(8,128)} %get-tuple-element.9.b, f32[16,1024]{1,0:T(8,128)} %get-tuple-element.10.c, f32[16,1024]{1,0:T(8,128)} %get-tuple-element.11.d), custom_call_target="tpu_custom_call" | custom-call | tf_op jit(solution)/shard_map/results/pallas_call | solution.py:642
